TPU v7x, 256 devices: a whole 4x4x8 slice. The times are simulated.
256 devices in a mesh: seq: 16 (over z_lo, x), dp: 16 (over z_hi, y, core).
Axes of the slice: x: 4, y: 4, z: 8 (z_hi: 2, z_lo: 4; z = z_hi * 4 + z_lo), core: 2. Of those that a mesh axis runs over, the one named last changes fastest.
Arguments:
- bases: int32 [65536], P(('dp', 'seq')), parts along dimension 0, may hold values from 0 to 3
- targets: int32 [16384, 128], P(('dp', 'seq')), parts along dimension 0, may hold values from 0 to 4
- w_conv: float32 [60, 768], replicated, may hold values from -1.5 to 1.5
- w_query: float32 [768, 512], replicated, may hold values from -12.5 to 12.5
- w_key: float32 [768, 512], replicated, may hold values from -0.31 to 0.31
- w_value: float32 [768, 512], replicated, may hold values from -0.21875 to 0.21875
- w_out: float32 [512, 768], replicated, may hold values from -0.25 to 0.25
- w_head: float32 [768, 128], replicated, may hold values from -0.21875 to 0.21875
Outputs:
- log_rate: float32 [16384, 128], P(('dp', 'seq')), parts along dimension 0
- d_conv: float32 [960, 768], P('dp', 'seq'), parts along dimension 0
- d_query: float32 [12288, 512], P(('dp', 'seq')), parts along dimension 0
- d_key: float32 [12288, 512], P(('dp', 'seq')), parts along dimension 0
- d_value: float32 [12288, 512], P(('dp', 'seq')), parts along dimension 0
- d_out: float32 [8192, 768], P(('dp', 'seq')), parts along dimension 0
- d_head: float32 [12288, 128], P(('dp', 'seq')), parts along dimension 0
There are 16 independent parts, one for each index of `dp`. A program takes and returns all parts, laid end to end along the dimension named above; an argument that names none is the same for every part. Nothing has to cross between parts.
All inputs are finite; a program needn't handle non-finite values.
Results may differ from a plain program's by a relative error of at most 0.0003.
Values sent between devices are 32-bit elements; how exact they have to be, the bound alone decides.
No kernel may reach another device: no remote copies, remote signals or barrier semaphores. Data moves between devices by JAX's collectives and lax.ppermute only.
A program may use at most 128 MiB of HBM per device.

v0:
```python
import math

import jax
import jax.numpy as jnp
from jax import lax
from jax.sharding import PartitionSpec as P

KW = 15
HEADS = 8
POOL = 4


def padded_2(value, sides, width):
    for axis, dim in sides:
        size, length = (lax.axis_size(axis), value.shape[dim])
        up = [(i, (i + 1) % size) for i in range(size - 1)]
        down = [(j, i) for i, j in up]
        last = lax.slice_in_dim(value, length - width, length, axis=dim)
        first = lax.slice_in_dim(value, 0, width, axis=dim)
        before = lax.ppermute(last, axis, up)
        after = lax.ppermute(first, axis, down)
        value = jnp.concatenate([before, value, after], axis=dim)
    return value


def matmul(left, right):
    return jnp.dot(left, right, precision=lax.Precision.HIGHEST)


def rms_norm(values):
    return values * lax.rsqrt(jnp.mean(values * values, axis=-1, keepdims=True) + 1e-06)


def einsum_high(form, left, right):
    return jnp.einsum(form, left, right, precision=lax.Precision.HIGHEST)


def per_device(bases, targets, w_conv, w_query, w_key, w_value, w_out, w_head):
    onehot = jax.nn.one_hot(bases, 4, dtype=jnp.float32)
    padded = padded_2(onehot, (("seq", 0),), KW // 2)
    local_len = bases.shape[0]
    columns = jnp.concatenate([padded[j : j + local_len] for j in range(KW)], axis=1)
    tokens = local_len // POOL
    head_size = w_query.shape[1] // HEADS
    score_scale = head_size ** (-0.5)
    keys_total = tokens * lax.axis_size("seq")

    def encode(wc, wq, wk, wv):
        pooled = jax.nn.gelu(matmul(columns, wc)).reshape(tokens, POOL, -1).mean(axis=1)
        normed = rms_norm(pooled)
        return (pooled, matmul(normed, wq), matmul(normed, wk), matmul(normed, wv))

    (pooled, queries, keys_here, values_here), encode_back = jax.vjp(
        encode, w_conv, w_query, w_key, w_value
    )
    query_heads = queries.reshape(tokens, HEADS, head_size).transpose(1, 0, 2)
    row_max = jnp.full((HEADS, tokens), -1e30, jnp.float32)
    key_block = lax.all_gather(keys_here, "seq", axis=0, tiled=True)
    value_block = lax.all_gather(values_here, "seq", axis=0, tiled=True)
    count = key_block.shape[0]
    key_heads = key_block.reshape(count, HEADS, head_size)
    value_heads = value_block.reshape(count, HEADS, head_size)
    scores = einsum_high("hqd,khd->hqk", query_heads, key_heads) * score_scale
    new_max = jnp.maximum(row_max, jnp.max(scores, axis=-1))
    probs = jnp.exp(scores - new_max[..., None])
    weight_sum = jnp.sum(probs, axis=-1)
    accum = einsum_high("hqk,khd->hqd", probs, value_heads)
    folded = (new_max, weight_sum, accum)
    row_max, weight_sum, accum = folded
    out_heads = accum / weight_sum[..., None]
    log_total = row_max + jnp.log(weight_sum)
    attended = out_heads.transpose(1, 0, 2).reshape(tokens, -1)

    def decode_tracks(attn_rows, pooled_rows, wo, wh):
        summed = pooled_rows + matmul(attn_rows, wo)
        return matmul(rms_norm(summed), wh)

    log_rate, decode_back = jax.vjp(decode_tracks, attended, pooled, w_out, w_head)
    grad_rate = (jnp.exp(log_rate) - targets.astype(jnp.float32)) / math.sqrt(keys_total)
    grad_attended, grad_pooled, grad_out, grad_head = decode_back(grad_rate)
    grad_heads = grad_attended.reshape(tokens, HEADS, head_size).transpose(1, 0, 2)
    row_delta = jnp.sum(grad_heads * out_heads, axis=-1)
    key_block = lax.all_gather(keys_here, "seq", axis=0, tiled=True)
    value_block = lax.all_gather(values_here, "seq", axis=0, tiled=True)
    count = key_block.shape[0]
    key_heads = key_block.reshape(count, HEADS, head_size)
    value_heads = value_block.reshape(count, HEADS, head_size)
    scores = einsum_high("hqd,khd->hqk", query_heads, key_heads) * score_scale
    probs = jnp.exp(scores - log_total[..., None])
    grad_probs = einsum_high("hqd,khd->hqk", grad_heads, value_heads)
    grad_scores = probs * (grad_probs - row_delta[..., None])
    grad_query = einsum_high("hqk,khd->hqd", grad_scores, key_heads) * score_scale
    key_part = (
        einsum_high("hqk,hqd->khd", grad_scores, query_heads).reshape(count, -1) * score_scale
    )
    value_part = einsum_high("hqk,hqd->khd", probs, grad_heads).reshape(count, -1)
    key_grads_all = key_part
    value_grads_all = value_part
    folded_grads = (grad_query, key_grads_all, value_grads_all)
    grad_query, key_grads_all, value_grads_all = folded_grads
    grad_keys, grad_values = (
        lax.psum_scatter(key_grads_all, "seq", scatter_dimension=0, tiled=True),
        lax.psum_scatter(value_grads_all, "seq", scatter_dimension=0, tiled=True),
    )
    grad_queries = grad_query.transpose(1, 0, 2).reshape(tokens, -1)
    grad_conv, grad_wq, grad_wk, grad_wv = encode_back(
        (grad_pooled, grad_queries, grad_keys, grad_values)
    )
    shares = (
        lax.psum_scatter(grad_conv, "seq", scatter_dimension=1, tiled=True),
        lax.psum_scatter(grad_wq, "seq", scatter_dimension=0, tiled=True),
        lax.psum_scatter(grad_wk, "seq", scatter_dimension=0, tiled=True),
        lax.psum_scatter(grad_wv, "seq", scatter_dimension=0, tiled=True),
        lax.psum_scatter(grad_out, "seq", scatter_dimension=0, tiled=True),
        lax.psum_scatter(grad_head, "seq", scatter_dimension=0, tiled=True),
    )
    return (log_rate, shares[0], shares[1], shares[2], shares[3], shares[4], shares[5])


def solution(mesh):
    placed = (P(("dp", "seq")), P(("dp", "seq"), None), P(), P(), P(), P(), P(), P())
    return jax.shard_map(
        per_device,
        mesh=mesh,
        in_specs=placed,
        out_specs=(
            P(("dp", "seq"), None),
            P("dp", "seq"),
            P(("dp", "seq"), None),
            P(("dp", "seq"), None),
            P(("dp", "seq"), None),
            P(("dp", "seq"), None),
            P(("dp", "seq"), None),
        ),
        check_vma=False,
    )
```

profile of v0, /device:TPU:16, one launch (start us, length us, event | category | flops | bytes accessed | tf_op | source)
XLA Modules:
  0.0 904.8 jit_solution(13134521493070872277)
XLA Ops:
  8.1 3.4 collective-permute-start
  12.9 4.1 collective-permute-done.1
  21.4 3.2 fusion.45
  24.7 3.2 fusion.43
  27.9 3.3 fusion.47
  31.3 81.1 %all-gather.3.cloned.1.call-done = f32[1024,512]{1,0:T(8,128)} async-done(((f32[64,512]{1,0:T(8,128)}), f32[1024,512]{1,0:T(8,128)}) %all-gather.3.cloned.1.call-update) | async-done | bytes 2097168 | tf_op jit(solution)/shard_map/all_gather | solution.py:58
  115.4 3.7 fusion.82
  121.1 74.6 %all-gather.5.cloned.1.call-done = f32[1024,512]{1,0:T(8,128)} async-done(((f32[64,512]{1,0:T(8,128)}), f32[1024,512]{1,0:T(8,128)}) %all-gather.5.cloned.1.call-update) | async-done | bytes 2097168 | tf_op jit(solution)/shard_map/all_gather | solution.py:59
  198.7 4.6 bitcast_divide_fusion
  207.8 3.5 fusion.2
  214.5 4.5 subtract_multiply_fusion
  219.1 3.3 convolution_multiply_fusion
  228.5 3.6 fusion.84
  232.1 4.3 fusion.3
  241.3 59.3 %reduce-scatter.25.cloned.1.call-done = f32[64,512]{1,0:T(8,128)} async-done(((f32[1024,512]{1,0:T(8,128)}), f32[64,512]{1,0:T(8,128)}) %reduce-scatter.25.cloned.1.call-update) | async-done | bytes 131088
  300.6 3.8 fusion.83
  304.4 82.7 %reduce-scatter.27.cloned.1.call-done = f32[64,512]{1,0:T(8,128)} async-done(((f32[1024,512]{1,0:T(8,128)}), f32[64,512]{1,0:T(8,128)}) %reduce-scatter.27.cloned.1.call-update) | async-done | bytes 131088
  392.4 3.7 fusion.12
  401.6 68.4 %reduce-scatter.23.cloned.1.call-done = f32[48,128]{1,0:T(8,128)} async-done(((f32[768,128]{1,0:T(8,128)}), f32[48,128]{1,0:T(8,128)}) %reduce-scatter.23.cloned.1.call-update) | async-done | bytes 24592 | tf_op jit(solution)/shard_map/reduce_scatter | solution.py:115
  470.1 86.2 %reduce-scatter.21.cloned.1.call-done = f32[32,768]{1,0:T(8,128)} async-done(((f32[512,768]{1,0:T(8,128)}), f32[32,768]{1,0:T(8,128)}) %reduce-scatter.21.cloned.1.call-update) | async-done | bytes 98320 | tf_op jit(solution)/shard_map/reduce_scatter | solution.py:114
  556.3 85.9 %reduce-scatter.15.cloned.1.call-done = f32[48,512]{1,0:T(8,128)} async-done(((f32[768,512]{1,0:T(8,128)}), f32[48,512]{1,0:T(8,128)}) %reduce-scatter.15.cloned.1.call-update) | async-done | bytes 98320 | tf_op jit(solution)/shard_map/reduce_scatter | solution.py:111
  642.2 83.3 %reduce-scatter.13.cloned.1.call-done = f32[60,48]{0,1:T(8,128)} async-done(((f32[60,768]{0,1:T(8,128)}), f32[60,48]{0,1:T(8,128)}) %reduce-scatter.13.cloned.1.call-update) | async-done | bytes 11536 | tf_op jit(solution)/shard_map/reduce_scatter | solution.py:110
  725.5 86.2 %reduce-scatter.17.cloned.1.call-done = f32[48,512]{1,0:T(8,128)} async-done(((f32[768,512]{1,0:T(8,128)}), f32[48,512]{1,0:T(8,128)}) %reduce-scatter.17.cloned.1.call-update) | async-done | bytes 98320 | tf_op jit(solution)/shard_map/reduce_scatter | solution.py:112
  811.7 85.8 %reduce-scatter.19.cloned.1.call-done = f32[48,512]{1,0:T(8,128)} async-done(((f32[768,512]{1,0:T(8,128)}), f32[48,512]{1,0:T(8,128)}) %reduce-scatter.19.cloned.1.call-update) | async-done | bytes 98320 | tf_op jit(solution)/shard_map/reduce_scatter | solution.py:113
  (104 shorter events, 44.1 us)
Async XLA Ops:
  7.2 196.1 %copy-start = (f32[512,768]{1,0:T(8,128)S(1)}, f32[512,768]{1,0:T(8,128)}, u32[]{:S(2)}) copy-start(f32[512,768]{1,0:T(8,128)} %param.14) | copy-start | bytes 4718596
  7.2 105.2 %all-gather.3.cloned.1.call-start = ((), (), s32[]{:S(2)}) async-start(), calls=%async_computation.8 | async-start | bytes 2228224 | tf_op jit(solution)/shard_map/all_gather | solution.py:58
  8.1 4.7 collective-permute-start
  11.5 5.5 collective-permute-start.1
  20.8 7.2 copy-start.4
  20.9 10.4 %copy-start.21 = (f32[64]{0:T(128)}, f32[64]{0:T(128)S(1)}, u32[]{:S(2)}) copy-start(f32[64]{0:T(128)S(1)} %multiply_reduce_fusion.4) | copy-start | bytes 772
  24.6 171.1 %all-gather.5.cloned.1.call-start = ((), (), s32[]{:S(2)}) async-start(), calls=%async_computation.9 | async-start | bytes 2228224 | tf_op jit(solution)/shard_map/all_gather | solution.py:59
  27.9 272.7 %reduce-scatter.25.cloned.1.call-start = ((), (), s32[]{:S(2)}) async-start(), calls=%async_computation.16 | async-start | bytes 2228224
  204.9 6.4 copy-start.15
  207.8 3.5 copy-start.8
  214.2 172.8 %reduce-scatter.27.cloned.1.call-start = ((), (), s32[]{:S(2)}) async-start(), calls=%async_computation.17 | async-start | bytes 2228224
  214.5 4.6 copy-start.7
  219.1 3.3 copy-start.3
  225.4 244.7 %reduce-scatter.23.cloned.1.call-start = ((), (), s32[]{:S(2)}) async-start(), calls=%async_computation.15 | async-start | bytes 417792 | tf_op jit(solution)/shard_map/reduce_scatter | solution.py:115
  228.4 327.9 %reduce-scatter.21.cloned.1.call-start = ((), (), s32[]{:S(2)}) async-start(), calls=%async_computation.14 | async-start | bytes 1671168 | tf_op jit(solution)/shard_map/reduce_scatter | solution.py:114
  232.1 410.1 %reduce-scatter.15.cloned.1.call-start = ((), (), s32[]{:S(2)}) async-start(), calls=%async_computation.11 | async-start | bytes 1671168 | tf_op jit(solution)/shard_map/reduce_scatter | solution.py:111
  238.3 62.3 %copy-start.11 = (f32[64,512]{1,0:T(8,128)}, f32[64,512]{1,0:T(8,128)S(1)}, u32[]{:S(2)}) copy-start(f32[64,512]{1,0:T(8,128)S(1)} %reshape.97) | copy-start | bytes 393220
  241.0 484.4 %reduce-scatter.13.cloned.1.call-start = ((), (), s32[]{:S(2)}) async-start(), calls=%async_computation.10 | async-start | bytes 417792 | tf_op jit(solution)/shard_map/reduce_scatter | solution.py:110
  304.4 87.5 %copy-start.22 = (f32[64]{0:T(128)S(1)}, f32[64]{0:T(128)}, u32[]{:S(2)}) copy-start(f32[64]{0:T(128)} %copy-done.21) | copy-start | bytes 772
  304.4 87.5 %copy-start.6 = (f32[64,768]{1,0:T(8,128)S(1)}, f32[64,768]{1,0:T(8,128)}, u32[]{:S(2)}) copy-start(f32[64,768]{1,0:T(8,128)} %copy-done.5) | copy-start | bytes 589828
  304.4 87.5 %copy-start.20 = (f32[64]{0:T(128)S(1)}, f32[64]{0:T(128)}, u32[]{:S(2)}) copy-start(f32[64]{0:T(128)} %get-tuple-element.23) | copy-start | bytes 772
  392.4 3.8 copy-start.13
  396.2 415.5 %reduce-scatter.17.cloned.1.call-start = ((), (), s32[]{:S(2)}) async-start(), calls=%async_computation.12 | async-start | bytes 1671168 | tf_op jit(solution)/shard_map/reduce_scatter | solution.py:112
  398.9 498.6 %reduce-scatter.19.cloned.1.call-start = ((), (), s32[]{:S(2)}) async-start(), calls=%async_computation.13 | async-start | bytes 1671168 | tf_op jit(solution)/shard_map/reduce_scatter | solution.py:113
  (11 other events, 21.3 us)
Sparse Core Ops, SparseCore 0:
  24.7 87.5 all-gather.2
  114.2 81.4 all-gather.4
  214.4 86.1 reduce-scatter.24
  303.0 84.0 reduce-scatter.26
  390.0 80.0 reduce-scatter.22
  473.2 83.0 reduce-scatter.20
  559.4 82.7 reduce-scatter.14
  645.4 79.9 reduce-scatter.12
  728.6 83.0 reduce-scatter.16
  814.8 82.6 reduce-scatter.18
where the time goes:
time: 910 us; the launch traced here: 905 us
  waiting for transfers between devices  798 us (88%)
  matrix products  66.2 us (7%)
  local copies, waits for them, and re-layouts  17.4 us (2%)
  between operations  15 us (2%)
    unnamed x12, waiting for transfers between devices  142 us
    reduce_scatter x1, waiting for transfers between devices, per_device(): lax.psum_scatter(grad_out, 'seq', scatter_dimension=0, tiled=True)  86.2 us
    reduce_scatter x1, waiting for transfers between devices, per_device(): lax.psum_scatter(grad_wk, 'seq', scatter_dimension=0, tiled=True)  86.2 us
    reduce_scatter x1, waiting for transfers between devices, per_device(): lax.psum_scatter(grad_wq, 'seq', scatter_dimension=0, tiled=True)  85.9 us
    reduce_scatter x1, waiting for transfers between devices, per_device(): lax.psum_scatter(grad_wv, 'seq', scatter_dimension=0, tiled=True)  85.8 us
    reduce_scatter x1, waiting for transfers between devices, per_device(): lax.psum_scatter(grad_conv, 'seq', scatter_dimension=1, tiled=True)  83.3 us
    all_gather x1, waiting for transfers between devices, per_device(): key_block = lax.all_gather(keys_here, 'seq', axis=0, tiled=True)  81.1 us
    all_gather x1, waiting for transfers between devices, per_device(): value_block = lax.all_gather(values_here, 'seq', axis=0, tiled=True)  74.6 us
  transfers between devices with their start and end apart: 12, of which 11 were waited for; matrix products, arithmetic and copies ran while one was open for 6% of the time, Pallas kernels for 0%

commit v1 on v0

v1 whole, which is shorter than its diff:
```python
import math

import jax
import jax.numpy as jnp
from jax import lax
from jax.experimental import pallas as pl
from jax.experimental.pallas import tpu as pltpu
from jax.sharding import PartitionSpec as P


C = 768
KW = 15
HEADS = 8
HS = 64
TRACKS = 128
POOL = 4
HD = 512
TOKENS = 1024
GROUP = 8
OWN = 64
F32 = jnp.float32
BF16 = jnp.bfloat16
GELU_A = math.sqrt(2.0 / math.pi)
GELU_B = GELU_A * 0.044715
WIN = 80
TILE = 256

VMEM = pl.BlockSpec(memory_space=pltpu.VMEM)
SMEM = pl.BlockSpec(memory_space=pltpu.SMEM)
ANY = pl.BlockSpec(memory_space=pl.ANY)


def dot(left, right):
    return lax.dot_general(left, right, (((1,), (0,)), ((), ())), preferred_element_type=F32)


def split2(a):
    hi = a.astype(BF16)
    return hi, (a - hi.astype(F32)).astype(BF16)


def split3(a):
    hi = a.astype(BF16)
    rest = a - hi.astype(F32)
    mid = rest.astype(BF16)
    return hi, mid, (rest - mid.astype(F32)).astype(BF16)


def dot3(left, right):
    lh, ll = split2(left)
    rh, rl = split2(right)
    return dot(lh, rh) + (dot(lh, rl) + dot(ll, rh))


def dot3_narrow(left, right):
    lh, ll = split2(left)
    rh, rl = split2(right)
    n = right.shape[1]
    both = dot(lh, jnp.concatenate([rh, rl], axis=1))
    return both[:, :n] + (both[:, n:] + dot(ll, rh))


def dot3_short(left, right):
    lh, ll = split2(left)
    rh, rl = split2(right)
    n = left.shape[0]
    both = dot(jnp.concatenate([lh, ll], axis=0), rh)
    return both[:n] + (both[n:] + dot(lh, rl))


def dot3_thin(left, right):
    lh, ll = split2(left)
    rh, rl = split2(right)
    return dot(jnp.concatenate([lh, lh, ll], axis=1), jnp.concatenate([rh, rl, rh], axis=0))


def dot6(left, right):
    lh, lm, ll = split3(left)
    rh, rm, rl = split3(right)
    return dot(lh, rh) + ((dot(lh, rm) + dot(lm, rh)) + (dot(lm, rm) + (dot(lh, rl) + dot(ll, rh))))


def rms_scale(a):
    return lax.rsqrt(jnp.mean(a * a, axis=-1, keepdims=True) + 1e-06)


def conv_weights(w_ref, pad_ref, out_ref):
    pad_ref[...] = jnp.zeros_like(pad_ref)
    for r in range(POOL):
        pad_ref[r, 4 * (r + 1):4 * (r + 1) + 4 * KW, :] = w_ref[...]
    for r in range(POOL):
        pieces = split3(pad_ref[r])
        zeros = jnp.zeros((256 - 3 * WIN, C), BF16)
        out_ref[:, r * C:(r + 1) * C] = jnp.concatenate([*pieces, zeros], axis=0)


def key_stack(k):
    h, m, l = split3(k)
    return jnp.concatenate([h, m, l, h, m, h], axis=1)


def query_stack(q_t):
    h, m, l = split3(q_t)
    return jnp.concatenate([h, h, h, m, m, l], axis=0)


def attend_kernel(
    info, bases, w_conv, wq_hbm, wk_hbm, wv_hbm,
    xh_out, xl_out, x_own, hot_own, qkv_out, o_out,
    pad, w_all, window, slabs, x_all, hot_all, sems,
):
    half, m = info[0], info[1]
    copies = []
    for i, w in enumerate((wq_hbm, wk_hbm, wv_hbm)):
        lanes = pl.ds(pl.multiple_of(lax.div(m, 2) * 128, 128), 128)
        copies.append(pltpu.make_async_copy(w.at[:, lanes], slabs.at[i], sems.at[i]))
    for copy in copies:
        copy.start()
    conv_weights(w_conv, pad, w_all)

    lane = lax.broadcasted_iota(jnp.int32, (128, 256), 1)
    row = lax.broadcasted_iota(jnp.int32, (128, 256), 0)
    within = lax.rem(lane, WIN)
    place = lax.div(lax.rem(within, 16), 4)
    pick = jnp.where(lax.rem(row, 4) == place, 1.0, 0.0).astype(BF16)
    mine = lax.broadcasted_iota(jnp.int32, (32, 128), 0) == lax.div(lax.broadcasted_iota(jnp.int32, (32, 128), 1), 4)
    code = lax.rem(lax.broadcasted_iota(jnp.int32, (1, 256), 1), 4).astype(F32)
    window[0:8, :] = jnp.zeros((8, 256), F32)
    window[TOKENS + 8:TOKENS + 16, :] = jnp.zeros((8, 256), F32)
    for part in range(8):
        pieces = []
        for q in range(4 * part, 4 * part + 4):
            line = bases[q // 2, q % 2:q % 2 + 1, :].astype(F32)
            pieces.append(jnp.where(mine, jnp.broadcast_to(line, (32, 128)), 0.0))
        value = dot(jnp.concatenate(pieces, axis=0).astype(BF16), pick)
        window[8 + 128 * part:8 + 128 * part + 128, :] = jnp.where(value == code, 1.0, 0.0)

    shift = lax.div(lax.rem(lax.broadcasted_iota(jnp.int32, (TILE, 256), 1), WIN), 16)
    real = lax.broadcasted_iota(jnp.int32, (TILE, 256), 1) < 3 * WIN
    steps = TOKENS // TILE

    def encode(c, _):
        start = pl.multiple_of(lax.rem(c + half * (steps // 2), steps) * TILE, TILE)
        around = window[pl.ds(start, TILE + 16), :]
        hot = jnp.zeros((TILE, 256), F32)
        for d in range(5):
            hot = jnp.where(shift == d, around[6 + d:6 + d + TILE, :], hot)
        hot = jnp.where(real, hot, 0.0).astype(BF16)
        total = jnp.zeros((TILE, C), F32)
        for r in range(POOL):
            pre = dot(hot, w_all[:, r * C:(r + 1) * C])
            total += 0.5 * pre * (1.0 + jnp.tanh(pre * (GELU_A + GELU_B * (pre * pre))))
        x = total * (1.0 / POOL)
        here = pl.ds(pl.multiple_of(c * TILE, TILE), TILE)
        x_all[here, :] = x
        hot_all[here, :] = hot
        return 0

    lax.fori_loop(0, steps, encode, 0)
    for copy in copies:
        copy.wait()
    odd = lax.rem(m, 2) == 1
    w_qkv = jnp.concatenate([jnp.where(odd, slabs[i, :, HS:], slabs[i, :, :HS]) * (HS ** -0.5 if i == 0 else 1.0) for i in range(3)], axis=1)
    wh, wm, wl = split3(w_qkv)

    def project(c, _):
        here = pl.ds(pl.multiple_of(c * TILE, TILE), TILE)
        x = x_all[here, :]
        xn = x * rms_scale(x)
        h, mid, low = split3(xn)
        xh_out[here, :] = h
        xl_out[here, :] = mid
        qkv_out[here, :] = dot(h, wh) + ((dot(h, wm) + dot(mid, wh)) + (dot(mid, wm) + (dot(h, wl) + dot(low, wh))))
        return 0

    lax.fori_loop(0, steps, project, 0)
    for part in range(2):
        here = pl.ds(pl.multiple_of(part * 512 + m * OWN, OWN), OWN)
        x_own[part * OWN:(part + 1) * OWN, :] = x_all[here, :]
        hot_own[part * OWN:(part + 1) * OWN, :] = hot_all[here, :]

    qkv = qkv_out[...]
    q_t = query_stack(jnp.transpose(qkv[:, :HS]))
    keys = key_stack(qkv[:, HS:2 * HS])
    vh, vl = split2(jnp.transpose(qkv[:, 2 * HS:]))
    v_both = jnp.concatenate([vh, vl], axis=0)
    outs = []
    for c in range(steps):
        scores = dot(keys, q_t[:, c * TILE:(c + 1) * TILE])
        e = jnp.exp(scores - jnp.max(scores, axis=0, keepdims=True))
        total = jnp.sum(e, axis=0, keepdims=True)
        eh, el = split2(e)
        both = dot(v_both, eh)
        outs.append(jnp.transpose((both[:HS] + (both[HS:] + dot(vh, el))) / total))
    o_out[...] = jnp.concatenate(
        [jnp.concatenate(outs[:steps // 2], axis=0), jnp.concatenate(outs[steps // 2:], axis=0)], axis=1
    )


def decode_kernel(
    info, o_parts, x_own, targets_here, targets_there, w_out, w_head,
    log_rate, do_out, dy_out, grads_out, yn_all,
):
    half = info[0]
    parts = [o_parts[h * OWN:(h + 1) * OWN, :] for h in range(HEADS)]
    attended = jnp.concatenate(
        [jnp.concatenate([p[:, :HS] for p in parts], axis=1), jnp.concatenate([p[:, HS:] for p in parts], axis=1)], axis=0
    )
    wout = w_out[...]
    wouth, woutl = split2(wout)
    ah, al = split2(attended)
    both = dot(jnp.concatenate([ah, al], axis=0), wouth)
    y = x_own[...] + (both[:2 * OWN] + (both[2 * OWN:] + dot(ah, woutl)))
    scale = rms_scale(y)
    yn = y * scale
    yn_all[...] = yn
    rate = dot3_narrow(yn, w_head[...])
    log_rate[...] = rate[:OWN]
    targets = jnp.concatenate([targets_here[...], targets_there[...]], axis=0).astype(F32)
    d_rate = (jnp.exp(rate) - targets) * (1.0 / math.sqrt(TOKENS))
    d_yn = dot3_thin(d_rate, jnp.transpose(w_head[...]))
    dy = scale * (d_yn - yn * jnp.mean(d_yn * yn, axis=-1, keepdims=True))
    dy_out[...] = dy
    dth, dtl = split2(jnp.transpose(dy))
    both = dot(wouth, jnp.concatenate([dth, dtl], axis=1))
    do_out[...] = both[:, :2 * OWN] + (both[:, 2 * OWN:] + dot(woutl, dth))

    heads = o_parts[pl.ds(pl.multiple_of(half * 256, 256), 256), :]
    o_t = jnp.concatenate(
        [
            jnp.concatenate(
                [jnp.transpose(heads[h * OWN:(h + 1) * OWN, :])[:HS], jnp.transpose(heads[h * OWN:(h + 1) * OWN, :])[HS:]], axis=1
            )
            for h in range(4)
        ],
        axis=0,
    )
    d_out = dot3_thin(o_t, dy)
    yn_half = yn_all[:, pl.ds(pl.multiple_of(half * 384, 128), 384)]
    d_head = dot3_thin(jnp.transpose(yn_half), d_rate)
    for p in range(GROUP):
        for j in range(6):
            grads_out[p * 240 + 32 * j:p * 240 + 32 * j + 32, :] = d_out[32 * p:32 * p + 32, 128 * j:128 * j + 128]
        grads_out[p * 240 + 192:p * 240 + 240, :] = d_head[48 * p:48 * p + 48, :]


def attend_back_kernel(info, do_parts, qkv_ref, xh_hbm, xl_hbm, sent, xh, xl, do_all, g_t, dk_acc, dv_acc, sems):
    half = info[0]
    lanes = pl.ds(pl.multiple_of(half * 384, 128), 384)
    copies = [
        pltpu.make_async_copy(xh_hbm.at[:, lanes], xh, sems.at[0]),
        pltpu.make_async_copy(xl_hbm.at[:, lanes], xl, sems.at[1]),
    ]
    for copy in copies:
        copy.start()
    for p in range(GROUP):
        both = jnp.transpose(do_parts[p * OWN:(p + 1) * OWN, :])
        do_all[p * OWN:(p + 1) * OWN, :] = both[:OWN]
        do_all[512 + p * OWN:512 + (p + 1) * OWN, :] = both[OWN:]
    qkv = qkv_ref[...]
    q = qkv[:, :HS]
    k = qkv[:, HS:2 * HS]
    v = qkv[:, 2 * HS:]
    q_t = query_stack(jnp.transpose(q))
    keys = key_stack(k)
    kh, kl = split2(jnp.transpose(k))
    k_both = jnp.concatenate([kh, kl], axis=0)
    vh, vl = split2(v)
    v_three = jnp.concatenate([vh, vh, vl], axis=1)
    do = do_all[...]
    dth, dtl = split2(jnp.transpose(do))
    do_t = jnp.concatenate([dth, dtl, dth], axis=0)
    dh, dl = split2(do)
    do_both = jnp.concatenate([dh, dl], axis=1)
    qh, ql = split2(q)
    q_both = jnp.concatenate([qh, ql], axis=1)
    for c in range(TOKENS // TILE):
        here = slice(c * TILE, (c + 1) * TILE)
        scores = dot(keys, q_t[:, here])
        e = jnp.exp(scores - jnp.max(scores, axis=0, keepdims=True))
        p = e * (1.0 / jnp.sum(e, axis=0, keepdims=True))
        dp = dot(v_three, do_t[:, here])
        ds = p * (dp - jnp.sum(p * dp, axis=0, keepdims=True))
        ph, plow = split2(p)
        sh, sl = split2(ds)
        both = dot(k_both, sh)
        g_t[0:HS, here] = (both[:HS] + (both[HS:] + dot(kh, sl))) * (HS ** -0.5)
        both = dot(ph, do_both[here])
        dv = both[:, :HS] + (both[:, HS:] + dot(plow, dh[here]))
        both = dot(sh, q_both[here])
        dk = both[:, :HS] + (both[:, HS:] + dot(sl, qh[here]))
        if c == 0:
            dk_acc[...] = dk
            dv_acc[...] = dv
        else:
            dk_acc[...] += dk
            dv_acc[...] += dv
    g_t[HS:2 * HS, :] = jnp.transpose(dk_acc[...])
    g_t[2 * HS:3 * HS, :] = jnp.transpose(dv_acc[...])
    for p in range(GROUP):
        sent[p * 264:p * 264 + 192, :] = jnp.concatenate(
            [g_t[:, p * OWN:(p + 1) * OWN], g_t[:, 512 + p * OWN:512 + (p + 1) * OWN]], axis=1
        )
    for copy in copies:
        copy.wait()
    gh, gl = split2(g_t[...])
    both = dot(jnp.concatenate([gh, gl], axis=0), xh[...])
    d_w = jnp.transpose(both[:192] + (both[192:] + dot(gh, xl[...])))
    for p in range(GROUP):
        mine = d_w[48 * p:48 * p + 48, :]
        sent[p * 264 + 192:p * 264 + 240, :] = mine[:, :128]
        sent[p * 264 + 240:p * 264 + 264, :] = jnp.concatenate([mine[:24, 128:], mine[24:, 128:]], axis=1)


def encode_back_kernel(
    info, got, wq_hbm, wk_hbm, wv_hbm, w_conv, x_own, hot_own, dy,
    d_query, d_key, d_value, sent,
    pad, w_all, weights, slopes, dconv, sems,
):
    half = info[0]
    copies = [pltpu.make_async_copy(w, weights.at[i], sems.at[i]) for i, w in enumerate((wq_hbm, wk_hbm, wv_hbm))]
    for copy in copies:
        copy.start()
    conv_weights(w_conv, pad, w_all)
    hot = hot_own[...]
    for r in range(POOL):
        pre = dot(hot, w_all[:, r * C:(r + 1) * C])
        square = pre * pre
        t = jnp.tanh(pre * (GELU_A + GELU_B * square))
        slopes[:, r * C:(r + 1) * C] = 0.5 * (1.0 + t) + 0.5 * pre * (1.0 - t * t) * (GELU_A + 3.0 * GELU_B * square)
    for part, out in enumerate((d_query, d_key)):
        out[...] = jnp.concatenate([got[264 * h + 192:264 * h + 240, part * HS:(part + 1) * HS] for h in range(HEADS)], axis=1)
    rows = [got[264 * h + 240:264 * h + 264, :] for h in range(HEADS)]
    d_value[...] = jnp.concatenate([jnp.concatenate([r[:, :HS], r[:, HS:]], axis=0) for r in rows], axis=1)
    total = jnp.zeros((C, 2 * OWN), F32)
    for part in range(3):
        g = jnp.concatenate([got[264 * h + part * HS:264 * h + (part + 1) * HS, :] for h in range(HEADS)], axis=0)
        copies[part].wait()
        total += dot3_narrow(weights[part], g)
    d_xn = jnp.transpose(total)
    x = x_own[...]
    scale = rms_scale(x)
    xn = x * scale
    d_x = (dy[...] + scale * (d_xn - xn * jnp.mean(d_xn * xn, axis=-1, keepdims=True))) * (1.0 / POOL)
    hot_t = jnp.transpose(hot[:, :128].astype(F32)).astype(BF16)
    hot_two = jnp.concatenate([hot_t, hot_t], axis=1)
    summed = jnp.zeros((4 * KW, C), F32)
    for r in range(POOL):
        dh, dl = split2(d_x * slopes[:, r * C:(r + 1) * C])
        moved = dot(hot_two, jnp.concatenate([dh, dl], axis=0))
        summed += moved[4 * (r + 1):4 * (r + 1) + 4 * KW, :]
    dconv[...] = jnp.zeros_like(dconv)
    dconv[0:4 * KW, :] = summed
    sent[...] = jnp.transpose(dconv[:, pl.ds(pl.multiple_of(half * 384, 128), 384)])


def finish_kernel(parts, grads, d_conv, d_out, d_head):
    total = parts[0:48, :]
    for p in range(1, GROUP):
        total = total + parts[48 * p:48 * p + 48, :]
    padded = jnp.concatenate([total, jnp.zeros((80, 128), F32)], axis=0)
    d_conv[...] = jnp.transpose(padded)[:4 * KW, :48]
    d_out[...] = jnp.concatenate([grads[32 * j:32 * j + 32, :] for j in range(6)], axis=1)
    d_head[...] = grads[192:240, :]


def shape(*dims, dtype=F32):
    return jax.ShapeDtypeStruct(dims, dtype)


def params(mib=40):
    return pltpu.CompilerParams(vmem_limit_bytes=mib * 1024 * 1024)


def per_device(bases, targets, w_conv, w_query, w_key, w_value, w_out, w_head):
    s = lax.axis_index("seq")
    info = jnp.stack([lax.div(s, GROUP), lax.rem(s, GROUP)]).astype(jnp.int32)
    groups = [list(range(GROUP)), list(range(GROUP, 2 * GROUP))]

    def exchange(value):
        return lax.all_to_all(value, "seq", 0, 0, axis_index_groups=groups, tiled=True)

    targets_there = lax.ppermute(targets, "seq", [(i, i ^ GROUP) for i in range(2 * GROUP)])
    every = lax.all_to_all(jnp.broadcast_to(bases.reshape(1, 2, 128), (16, 2, 128)), "seq", 0, 0, tiled=True)

    xh, xl, x_own, hot_own, qkv, o_here = pl.pallas_call(
        attend_kernel,
        out_shape=(
            shape(TOKENS, C, dtype=BF16), shape(TOKENS, C, dtype=BF16), shape(2 * OWN, C), shape(2 * OWN, 256, dtype=BF16),
            shape(TOKENS, 3 * HS), shape(512, 128),
        ),
        in_specs=[SMEM, VMEM, VMEM, ANY, ANY, ANY],
        out_specs=(VMEM,) * 6,
        scratch_shapes=[
            pltpu.VMEM((POOL, WIN, C), F32),
            pltpu.VMEM((256, POOL * C), BF16),
            pltpu.VMEM((TOKENS + 16, 256), F32),
            pltpu.VMEM((3, C, 128), F32),
            pltpu.VMEM((TOKENS, C), F32),
            pltpu.VMEM((TOKENS, 256), BF16),
            pltpu.SemaphoreType.DMA((3,)),
        ],
        compiler_params=params(),
        name="attend",
    )(info, every, w_conv, w_query, w_key, w_value)

    log_rate, do_sent, dy, grads_part = pl.pallas_call(
        decode_kernel,
        out_shape=(shape(OWN, TRACKS), shape(HD, 128), shape(2 * OWN, C), shape(GROUP * 240, 128)),
        in_specs=[SMEM] + [VMEM] * 6,
        out_specs=(VMEM,) * 4,
        scratch_shapes=[pltpu.VMEM((2 * OWN, C), F32)],
        compiler_params=params(),
        name="decode",
    )(info, exchange(o_here), x_own, targets, targets_there, w_out, w_head)
    grads = lax.psum_scatter(grads_part, "seq", scatter_dimension=0, axis_index_groups=groups, tiled=True)

    sent = pl.pallas_call(
        attend_back_kernel,
        out_shape=shape(GROUP * 264, 128),
        in_specs=[SMEM, VMEM, VMEM, ANY, ANY],
        out_specs=VMEM,
        scratch_shapes=[
            pltpu.VMEM((TOKENS, 384), BF16),
            pltpu.VMEM((TOKENS, 384), BF16),
            pltpu.VMEM((TOKENS, HS), F32),
            pltpu.VMEM((3 * HS, TOKENS), F32),
            pltpu.VMEM((TOKENS, HS), F32),
            pltpu.VMEM((TOKENS, HS), F32),
            pltpu.SemaphoreType.DMA((2,)),
        ],
        compiler_params=params(),
        name="attend_back",
    )(info, exchange(do_sent), qkv, xh, xl)

    d_query, d_key, d_value, conv_sent = pl.pallas_call(
        encode_back_kernel,
        out_shape=(shape(48, HD), shape(48, HD), shape(48, HD), shape(GROUP * 48, 128)),
        in_specs=[SMEM, VMEM, ANY, ANY, ANY] + [VMEM] * 4,
        out_specs=(VMEM,) * 4,
        scratch_shapes=[
            pltpu.VMEM((POOL, WIN, C), F32),
            pltpu.VMEM((256, POOL * C), BF16),
            pltpu.VMEM((3, C, HD), F32),
            pltpu.VMEM((2 * OWN, POOL * C), F32),
            pltpu.VMEM((128, C), F32),
            pltpu.SemaphoreType.DMA((3,)),
        ],
        compiler_params=params(),
        name="encode_back",
    )(info, exchange(sent), w_query, w_key, w_value, w_conv, x_own, hot_own, dy)

    d_conv, d_out, d_head = pl.pallas_call(
        finish_kernel,
        out_shape=(shape(4 * KW, 48), shape(32, C), shape(48, TRACKS)),
        in_specs=[VMEM] * 2,
        out_specs=(VMEM,) * 3,
        compiler_params=params(16),
        name="finish",
    )(exchange(conv_sent), grads)
    return (log_rate, d_conv, d_query, d_key, d_value, d_out, d_head)


def solution(mesh):
    rows = P(("dp", "seq"), None)
    return jax.shard_map(
        per_device,
        mesh=mesh,
        in_specs=(P(("dp", "seq")), rows, P(), P(), P(), P(), P(), P()),
        out_specs=(rows, P("dp", "seq"), rows, rows, rows, rows, rows),
        check_vma=False,
    )
```

time: 910 us -> 151 us (0.17)
  waiting for transfers between devices: 798 us -> 45 us
  matrix products: 66.2 us -> 0 us
  Pallas kernels: 0 us -> 34.3 us
  starting transfers between devices: 5.55 us -> 21.5 us
  blocking collectives: 0 us -> 11 us
    reduce_scatter x6 -> x1, waiting for transfers between devices: 496 us -> 20.3 us  [per_device(): lax.psum_scatter(grads_part, 'seq', scatter_dimension=0, axis_index_group...]
    all_gather x2 -> x0, waiting for transfers between devices: 156 us -> none  [the longest x1 81.1 us: per_device(): key_block = lax.all_gather(keys_here, 'seq', axis=0, tiled=True)]
    unnamed x12 -> x1, waiting for transfers between devices: 142 us -> 0.46 us
    dot_general x22 -> x0, matrix products: 62.9 us -> none  [the longest x16 39 us: matmul(): return jnp.dot(left, right, precision=lax.Precision.HIGHEST)]
    pallas_call x0 -> x5, Pallas kernels: none -> 34.3 us  [the longest x1 15 us: per_device(): pl.pallas_call(attend_kernel, out_shape=(shape(TOKENS, C, dtype=BF16), sh...]
    all_to_all x0 -> x4, starting transfers between devices: none -> 20.7 us  [the longest x3 12.2 us: exchange(): lax.all_to_all(value, 'seq', 0, 0, axis_index_groups=groups, tiled=True)]
    all_to_all x0 -> x4, waiting for transfers between devices: none -> 19.6 us  [the longest x3 12.2 us: exchange(): lax.all_to_all(value, 'seq', 0, 0, axis_index_groups=groups, tiled=True)]
    unnamed x48 -> x59, local copies, waits for them, and re-layouts: 8.58 us -> 21.5 us
  transfers between devices with their start and end apart: 12 -> 6, of which waited for: 11 -> 5; matrix products, arithmetic and copies ran while one was open for 6% -> 0% of each run, Pallas kernels for 0% -> 3%
where the time goes in v1:
time: 151 us; the launch traced here: 149 us
  waiting for transfers between devices  45 us (30%)
  Pallas kernels  34.3 us (23%)
  local copies, waits for them, and re-layouts  22.8 us (15%)
  starting transfers between devices  21.5 us (14%)
  between operations  14.2 us (9%)
  blocking collectives  11 us (7%)
    unnamed x59, local copies, waits for them, and re-layouts  21.5 us
    reduce_scatter x1, waiting for transfers between devices, per_device(): lax.psum_scatter(grads_part, 'seq', scatter_dimension=0, axis_index_group...  20.3 us
    pallas_call x1, Pallas kernels, per_device(): pl.pallas_call(attend_kernel, out_shape=(shape(TOKENS, C, dtype=BF16), sh...  15 us
    all_to_all x3, starting transfers between devices, exchange(): lax.all_to_all(value, 'seq', 0, 0, axis_index_groups=groups, tiled=True)  12.2 us
    all_to_all x3, waiting for transfers between devices, exchange(): lax.all_to_all(value, 'seq', 0, 0, axis_index_groups=groups, tiled=True)  12.2 us
    all_to_all x1, blocking collectives, exchange(): lax.all_to_all(value, 'seq', 0, 0, axis_index_groups=groups, tiled=True)  11 us
    pallas_call x1, Pallas kernels, per_device(): pl.pallas_call(attend_back_kernel, out_shape=shape(GROUP * 264, 128), in_...  10.1 us
    all_to_all x1, starting transfers between devices, per_device(): lax.all_to_all(jnp.broadcast_to(bases.reshape(1, 2, 128), (16, 2, 128)),...  8.47 us
  transfers between devices with their start and end apart: 6, of which 5 were waited for; matrix products, arithmetic and copies ran while one was open for 0% of the time, Pallas kernels for 3%

profile of v1, /device:TPU:16, one launch (start us, length us, event | category | flops | bytes accessed | tf_op | source)
XLA Modules:
  0.0 149.4 jit_solution(6726542319877403832)
XLA Ops:
  7.2 1.3 broadcast_in_dim.8
  8.5 8.5 %all-to-all-start = ((s32[16,2,128]{2,1,0:T(2,128)}), s32[16,2,128]{2,1,0:T(2,128)S(1)}, u32[]{:S(2)}, u32[]{:S(2)}) async-start(s32[16,2,128]{2,1,0:T(2,128)} %broadcast_in_dim.8), calls=%async_computation | async-start | bytes 32768 | tf_op jit(solution)/shard_map/all_to_all | solution.py:384
  17.5 7.4 %all-to-all-done.bases = s32[16,2,128]{2,1,0:T(2,128)S(1)} async-done(((s32[16,2,128]{2,1,0:T(2,128)}), s32[16,2,128]{2,1,0:T(2,128)S(1)}, u32[]{:S(2)}, u32[]{:S(2)}) %all-to-all-start) | async-done | bytes 16416 | tf_op jit(solution)/shard_map/all_to_all | solution.py:384
  24.9 1.4 copy-done
  26.3 1.4 copy-done.2
  27.7 1.4 copy-done.4
  30.7 15.0 %attend.1 = (bf16[1024,768]{1,0:T(8,128)(2,1)S(1)}, bf16[1024,768]{1,0:T(8,128)(2,1)S(1)}, f32[128,768]{1,0:T(8,128)S(1)}, bf16[128,256]{1,0:T(8,128)(2,1)S(1)},...) custom-call(s32[2]{0:T(128)S(1)} %copy-done.26, s32[16,2,128]{2,1,0:T(2,128)S(1)} %all-to-all-done.bases, ...), custom_call_target="tpu_custom_call" | custom-call | tf_op jit(solution)/shard_map/attend/pallas_call | solution.py:386
  45.7 1.2 copy-done.8
  46.9 1.0 copy-done.10
  49.2 4.1 %all-to-all-start.1 = ((f32[8,64,128]{2,1,0:T(8,128)}), f32[8,64,128]{2,1,0:T(8,128)}, u32[]{:S(2)}, u32[]{:S(2)}) async-start(f32[8,64,128]{2,1,0:T(8,128)} %bitcast.14), calls=%async_computation.1 | async-start | bytes 524288 | tf_op jit(solution)/shard_map/all_to_all | solution.py:381
  53.8 4.7 %collective-permute-done.targets_there = s32[64,128]{1,0:T(8,128)S(1)} collective-permute-done((s32[64,128]{1,0:T(8,128)}, s32[64,128]{1,0:T(8,128)S(1)}, u32[]{:S(2)}, u32[]{:S(2)}) %collective-permute-start) | collective-permute-done | bytes 32800 | tf_op jit(solution)/shard_map/ppermute | solution.py:383
  59.1 1.4 all-to-all-done.1
  60.5 1.0 copy-done.15
  63.7 3.4 %decode.1 = (f32[64,128]{1,0:T(8,128)}, f32[512,128]{1,0:T(8,128)S(1)}, f32[128,768]{1,0:T(8,128)S(1)}, f32[1920,128]{1,0:T(8,128)S(1)}) custom-call(s32[2]{0:T(128)S(1)} %copy-done.27, f32[512,128]{1,0:T(8,128)} %bitcast.4.o_parts, f32[128,768]{1,0:T(8,128)S(1)} %get-tuple-element.25.x_own, s32[64,128]{1,0:T(8,128)S(1)} %copy-done.23, ...), custom_call_target="tpu_custom_call" | custom-call | tf_op jit(solution)/shard_map/decode/pallas_call | solution.py:407
  68.1 11.0 %all_to_all.49 = f32[8,64,128]{2,1,0:T(8,128)S(1)} all-to-all(f32[8,64,128]{2,1,0:T(8,128)S(1)} %bitcast.15), channel_id=1, replica_groups={{0,16,32,48,64,80,96,112},{128,144,160,176,192,208,224,240},{1,17,33,49..., dimensions={0} | all-to-all | bytes 524288 | tf_op jit(solution)/shard_map/all_to_all | solution.py:381
  79.1 10.1 %attend_back.1 = f32[2112,128]{1,0:T(8,128)S(1)} custom-call(s32[2]{0:T(128)S(1)} %copy-done.27, f32[512,128]{1,0:T(8,128)S(1)} %bitcast.12, f32[1024,192]{1,0:T(8,128)S(1)} %copy-done.11, bf16[1024,768]{1,0:T(8,128)(2,1)S(1)} %get-tuple-element.29.xh_hbm, bf16[1024,768]{1,0:T(8,128)(2,1)S(1)} %copy-done.9), custom_call_target="tpu_custom_call" | custom-call | tf_op jit(solution)/shard_map/attend_back/pallas_call | solution.py:418
  89.3 1.0 copy-done.6
  90.2 4.5 %all-to-all-start.3 = ((f32[8,264,128]{2,1,0:T(8,128)}), f32[8,264,128]{2,1,0:T(8,128)}, u32[]{:S(2)}, u32[]{:S(2)}) async-start(f32[8,264,128]{2,1,0:T(8,128)} %bitcast.11), calls=%async_computation.3 | async-start | bytes 2162688 | tf_op jit(solution)/shard_map/all_to_all | solution.py:381
  95.5 10.8 %all-to-all-done.3 = f32[8,264,128]{2,1,0:T(8,128)} async-done(((f32[8,264,128]{2,1,0:T(8,128)}), f32[8,264,128]{2,1,0:T(8,128)}, u32[]{:S(2)}, u32[]{:S(2)}) %all-to-all-start.3) | async-done | bytes 1081376 | tf_op jit(solution)/shard_map/all_to_all | solution.py:381
  106.3 1.4 copy-done.5
  108.6 1.0 copy-done.17
  110.5 5.2 %encode_back.1 = (f32[48,512]{1,0:T(8,128)}, f32[48,512]{1,0:T(8,128)}, f32[48,512]{1,0:T(8,128)}, f32[384,128]{1,0:T(8,128)S(1)}) custom-call(s32[2]{0:T(128)S(1)} %copy-done.28, f32[2112,128]{1,0:T(8,128)} %bitcast.8.got, f32[768,512]{1,0:T(8,128)S(1)} %copy-done.1, f32[768,512]{1,0:T(8,128)S(1)} %copy-done.3, f32[768,512]{1,0:T(8,128)S(1)} %copy-done.5, ...), custom_call_target="tpu_custom_call" | custom-call | tf_op jit(solution)/shard_map/encode_back/pallas_call | solution.py:436
  116.3 3.7 %all-to-all-start.4 = ((f32[8,48,128]{2,1,0:T(8,128)}), f32[8,48,128]{2,1,0:T(8,128)S(1)}, u32[]{:S(2)}, u32[]{:S(2)}) async-start(f32[8,48,128]{2,1,0:T(8,128)} %bitcast.16), calls=%async_computation.4 | async-start | bytes 393216 | tf_op jit(solution)/shard_map/all_to_all | solution.py:381
  120.0 20.3 %reduce-scatter.2.cloned.1.call-done.grads = f32[240,128]{1,0:T(8,128)} async-done(((f32[1920,128]{1,0:T(8,128)}), f32[240,128]{1,0:T(8,128)}) %reduce-scatter.2.cloned.1.call-update) | async-done | bytes 122896 | tf_op jit(solution)/shard_map/reduce_scatter | solution.py:416
  (56 shorter events, 13.3 us)
Async XLA Ops:
  8.5 16.5 %all-to-all-start = ((s32[16,2,128]{2,1,0:T(2,128)}), s32[16,2,128]{2,1,0:T(2,128)S(1)}, u32[]{:S(2)}, u32[]{:S(2)}) async-start(s32[16,2,128]{2,1,0:T(2,128)} %broadcast_in_dim.8), calls=%async_computation | async-start | bytes 32768 | tf_op jit(solution)/shard_map/all_to_all | solution.py:384
  24.9 1.4 copy-start
  26.3 1.4 copy-start.2
  27.7 1.4 copy-start.4
  29.2 0.9 copy-start.13
  30.7 29.8 %copy-start.7 = (f32[512,768]{1,0:T(8,128)S(1)}, f32[512,768]{1,0:T(8,128)}, u32[]{:S(2)}) copy-start(f32[512,768]{1,0:T(8,128)} %w_out.1) | copy-start | bytes 4718596
  45.7 1.2 copy-start.8
  46.9 1.0 copy-start.10
  49.2 11.3 %all-to-all-start.1 = ((f32[8,64,128]{2,1,0:T(8,128)}), f32[8,64,128]{2,1,0:T(8,128)}, u32[]{:S(2)}, u32[]{:S(2)}) async-start(f32[8,64,128]{2,1,0:T(8,128)} %bitcast.14), calls=%async_computation.1 | async-start | bytes 524288 | tf_op jit(solution)/shard_map/all_to_all | solution.py:381
  53.3 5.2 %collective-permute-start = (s32[64,128]{1,0:T(8,128)}, s32[64,128]{1,0:T(8,128)S(1)}, u32[]{:S(2)}, u32[]{:S(2)}) collective-permute-start(s32[64,128]{1,0:T(8,128)} %targets_here.1), channel_id=1, source_target_pairs={{0,128},{16,144},{32,160},{48,176},{64,192},{80,208},{96,224},{112... | collective-permute-start | bytes 98312 | tf_op jit(solution)/shard_map/ppermute | solution.py:383
  60.5 1.0 copy-start.15
  63.7 15.4 %copy-start.9 = (bf16[1024,768]{1,0:T(8,128)(2,1)S(1)}, bf16[1024,768]{1,0:T(8,128)(2,1)}, u32[]{:S(2)}) copy-start(bf16[1024,768]{1,0:T(8,128)(2,1)} %copy-done.8) | copy-start | bytes 4718596
  63.7 15.4 %copy-start.11 = (f32[1024,192]{1,0:T(8,128)S(1)}, f32[1024,192]{1,0:T(8,128)}, u32[]{:S(2)}) copy-start(f32[1024,192]{1,0:T(8,128)} %copy-done.10) | copy-start | bytes 2359300
  67.1 1.0 copy-start.12
  68.1 21.2 %copy-start.16 = (f32[128,768]{1,0:T(8,128)}, f32[128,768]{1,0:T(8,128)S(1)}, u32[]{:S(2)}) copy-start(f32[128,768]{1,0:T(8,128)S(1)} %get-tuple-element.32.dy) | copy-start | bytes 1179652
  89.2 1.0 copy-start.6
  90.2 16.0 %copy-start.1 = (f32[768,512]{1,0:T(8,128)S(1)}, f32[768,512]{1,0:T(8,128)}, u32[]{:S(2)}) copy-start(f32[768,512]{1,0:T(8,128)} %wq_hbm.3) | copy-start | bytes 4718596
  90.2 16.0 %copy-start.3 = (f32[768,512]{1,0:T(8,128)S(1)}, f32[768,512]{1,0:T(8,128)}, u32[]{:S(2)}) copy-start(f32[768,512]{1,0:T(8,128)} %wk_hbm.3) | copy-start | bytes 4718596
  90.2 16.0 %copy-start.28 = (s32[2]{0:T(128)S(1)}, s32[2]{0:T(128)}, u32[]{:S(2)}) copy-start(s32[2]{0:T(128)} %pad_add_fusion.info) | copy-start | bytes 28
  90.2 16.0 %all-to-all-start.3 = ((f32[8,264,128]{2,1,0:T(8,128)}), f32[8,264,128]{2,1,0:T(8,128)}, u32[]{:S(2)}, u32[]{:S(2)}) async-start(f32[8,264,128]{2,1,0:T(8,128)} %bitcast.11), calls=%async_computation.3 | async-start | bytes 2162688 | tf_op jit(solution)/shard_map/all_to_all | solution.py:381
  94.8 45.6 %reduce-scatter.2.cloned.1.call-start = ((), (), s32[]{:S(2)}) async-start(), calls=%async_computation.6 | async-start | bytes 1105920 | tf_op jit(solution)/shard_map/reduce_scatter | solution.py:416
  106.3 1.4 copy-start.5
  108.6 1.0 copy-start.17
  116.3 24.0 %all-to-all-start.4 = ((f32[8,48,128]{2,1,0:T(8,128)}), f32[8,48,128]{2,1,0:T(8,128)S(1)}, u32[]{:S(2)}, u32[]{:S(2)}) async-start(f32[8,48,128]{2,1,0:T(8,128)} %bitcast.16), calls=%async_computation.4 | async-start | bytes 393216 | tf_op jit(solution)/shard_map/all_to_all | solution.py:381
  (11 other events, 8.1 us)
Sparse Core Ops, SparseCore 0:
  98.1 42.1 reduce-scatter.1

commit v2 on v1

v2 whole, which is shorter than its diff:
```python
import math

import jax
import jax.numpy as jnp
from jax import lax
from jax.experimental import pallas as pl
from jax.experimental.pallas import tpu as pltpu
from jax.sharding import PartitionSpec as P


C = 768
KW = 15
HEADS = 8
HS = 64
TRACKS = 128
POOL = 4
HD = 512
TOKENS = 1024
GROUP = 8
OWN = 64
F32 = jnp.float32
BF16 = jnp.bfloat16
GELU_A = math.sqrt(2.0 / math.pi)
GELU_B = GELU_A * 0.044715
WIN = 80
TILE = 256

VMEM = pl.BlockSpec(memory_space=pltpu.VMEM)
SMEM = pl.BlockSpec(memory_space=pltpu.SMEM)
ANY = pl.BlockSpec(memory_space=pl.ANY)


def dot(left, right):
    return lax.dot_general(left, right, (((1,), (0,)), ((), ())), preferred_element_type=F32)


def split2(a):
    hi = a.astype(BF16)
    return hi, (a - hi.astype(F32)).astype(BF16)


def split3(a):
    hi = a.astype(BF16)
    rest = a - hi.astype(F32)
    mid = rest.astype(BF16)
    return hi, mid, (rest - mid.astype(F32)).astype(BF16)


def dot3(left, right):
    lh, ll = split2(left)
    rh, rl = split2(right)
    return dot(lh, rh) + (dot(lh, rl) + dot(ll, rh))


def dot3_narrow(left, right):
    lh, ll = split2(left)
    rh, rl = split2(right)
    n = right.shape[1]
    both = dot(lh, jnp.concatenate([rh, rl], axis=1))
    return both[:, :n] + (both[:, n:] + dot(ll, rh))


def dot3_short(left, right):
    lh, ll = split2(left)
    rh, rl = split2(right)
    n = left.shape[0]
    both = dot(jnp.concatenate([lh, ll], axis=0), rh)
    return both[:n] + (both[n:] + dot(lh, rl))


def dot3_thin(left, right):
    lh, ll = split2(left)
    rh, rl = split2(right)
    return dot(jnp.concatenate([lh, lh, ll], axis=1), jnp.concatenate([rh, rl, rh], axis=0))


def dot6(left, right):
    lh, lm, ll = split3(left)
    rh, rm, rl = split3(right)
    return dot(lh, rh) + ((dot(lh, rm) + dot(lm, rh)) + (dot(lm, rm) + (dot(lh, rl) + dot(ll, rh))))


def rms_scale(a):
    return lax.rsqrt(jnp.mean(a * a, axis=-1, keepdims=True) + 1e-06)


def conv_weights(w_ref, pad_ref, out_ref):
    pad_ref[...] = jnp.zeros_like(pad_ref)
    for r in range(POOL):
        pad_ref[r, 4 * (r + 1):4 * (r + 1) + 4 * KW, :] = w_ref[...]
    for r in range(POOL):
        pieces = split3(pad_ref[r])
        zeros = jnp.zeros((256 - 3 * WIN, C), BF16)
        out_ref[:, r * C:(r + 1) * C] = jnp.concatenate([*pieces, zeros], axis=0)


def key_stack(k):
    h, m, l = split3(k)
    return jnp.concatenate([h, m, l, h, m, h], axis=1)


def query_stack(q_t):
    h, m, l = split3(q_t)
    return jnp.concatenate([h, h, h, m, m, l], axis=0)


def attend_kernel(
    info, bases, w_conv, wq_hbm, wk_hbm, wv_hbm,
    xh_out, xl_out, scale_out, x_own, hot_t, qkv_out, w_t, inverse, o_out, slopes_hbm, eh_hbm, el_hbm,
    pad, w_all, window, slabs, x_all, slopes, eh_all, el_all, sems, slope_sems, e_sems,
):
    half, m = info[0], info[1]
    copies = []
    for i, w in enumerate((wq_hbm, wk_hbm, wv_hbm)):
        lanes = pl.ds(pl.multiple_of(lax.div(m, 2) * 128, 128), 128)
        copies.append(pltpu.make_async_copy(w.at[:, lanes], slabs.at[i], sems.at[i]))
    for copy in copies:
        copy.start()
    conv_weights(w_conv, pad, w_all)

    lane = lax.broadcasted_iota(jnp.int32, (128, 256), 1)
    row = lax.broadcasted_iota(jnp.int32, (128, 256), 0)
    within = lax.rem(lane, WIN)
    place = lax.div(lax.rem(within, 16), 4)
    pick = jnp.where(lax.rem(row, 4) == place, 1.0, 0.0).astype(BF16)
    mine = lax.broadcasted_iota(jnp.int32, (32, 128), 0) == lax.div(lax.broadcasted_iota(jnp.int32, (32, 128), 1), 4)
    code = lax.rem(lax.broadcasted_iota(jnp.int32, (1, 256), 1), 4).astype(F32)
    window[0:8, :] = jnp.zeros((8, 256), F32)
    window[TOKENS + 8:TOKENS + 16, :] = jnp.zeros((8, 256), F32)
    for part in range(8):
        pieces = []
        for q in range(4 * part, 4 * part + 4):
            line = bases[q // 2, q % 2:q % 2 + 1, :].astype(F32)
            pieces.append(jnp.where(mine, jnp.broadcast_to(line, (32, 128)), 0.0))
        value = dot(jnp.concatenate(pieces, axis=0).astype(BF16), pick)
        window[8 + 128 * part:8 + 128 * part + 128, :] = jnp.where(value == code, 1.0, 0.0)

    shift = lax.div(lax.rem(lax.broadcasted_iota(jnp.int32, (TILE, 256), 1), WIN), 16)
    real = lax.broadcasted_iota(jnp.int32, (TILE, 256), 1) < 3 * WIN
    steps = TOKENS // TILE

    def encode(c, _):
        start = pl.multiple_of(lax.rem(c + half * (steps // 2), steps) * TILE, TILE)
        around = window[pl.ds(start, TILE + 16), :]
        hot = jnp.zeros((TILE, 256), F32)
        for d in range(5):
            hot = jnp.where(shift == d, around[6 + d:6 + d + TILE, :], hot)
        hot = jnp.where(real, hot, 0.0).astype(BF16)
        here = pl.ds(pl.multiple_of(c * TILE, TILE), TILE)
        total = jnp.zeros((TILE, C), F32)
        for r in range(POOL):
            pre = dot(hot, w_all[:, r * C:(r + 1) * C])
            square = pre * pre
            t = jnp.tanh(pre * (GELU_A + GELU_B * square))
            near = 0.5 + 0.5 * t
            total += pre * near
            slopes[here, r * C:(r + 1) * C] = near + pre * (near * (1.0 - t)) * (GELU_A + 3.0 * GELU_B * square)
        x_all[here, :] = total * (1.0 / POOL)
        hot_t[:, here] = jnp.transpose(hot[:, :128].astype(F32)).astype(BF16)
        pltpu.make_async_copy(slopes.at[here], slopes_hbm.at[here], slope_sems.at[c]).start()
        return 0

    lax.fori_loop(0, steps, encode, 0)
    for copy in copies:
        copy.wait()
    odd = lax.rem(m, 2) == 1
    columns = [jnp.where(odd, slabs[i, :, HS:], slabs[i, :, :HS]) for i in range(3)]
    w_t[...] = jnp.transpose(jnp.concatenate(columns, axis=1))
    w_qkv = jnp.concatenate([columns[0] * HS ** -0.5, columns[1], columns[2]], axis=1)
    wh, wm, wl = split3(w_qkv)

    def project(c, _):
        here = pl.ds(pl.multiple_of(c * TILE, TILE), TILE)
        x = x_all[here, :]
        scale = rms_scale(x)
        scale_out[here, :] = jnp.broadcast_to(scale, (TILE, 128))
        xn = x * scale
        h, mid, low = split3(xn)
        xh_out[here, :] = h
        xl_out[here, :] = mid
        qkv_out[here, :] = dot(h, wh) + ((dot(h, wm) + dot(mid, wh)) + (dot(mid, wm) + (dot(h, wl) + dot(low, wh))))
        return 0

    lax.fori_loop(0, steps, project, 0)
    for part in range(2):
        here = pl.ds(pl.multiple_of(part * 512 + m * OWN, OWN), OWN)
        x_own[part * OWN:(part + 1) * OWN, :] = x_all[here, :]

    qkv = qkv_out[...]
    q_t = query_stack(jnp.transpose(qkv[:, :HS]))
    keys = key_stack(qkv[:, HS:2 * HS])
    vh, vl = split2(jnp.transpose(qkv[:, 2 * HS:]))
    v_both = jnp.concatenate([vh, vl], axis=0)
    outs = []
    for c in range(steps):
        scores = dot(keys, q_t[:, c * TILE:(c + 1) * TILE])
        e = jnp.exp(scores - jnp.max(scores, axis=0, keepdims=True))
        eh, el = split2(e)
        over = 1.0 / jnp.sum(eh.astype(F32) + el.astype(F32), axis=0, keepdims=True)
        inverse[:, c * TILE:(c + 1) * TILE] = over
        eh_all[c] = eh
        el_all[c] = el
        for i, (here, there) in enumerate(((eh_all, eh_hbm), (el_all, el_hbm))):
            pltpu.make_async_copy(here.at[c], there.at[c], e_sems.at[i, c]).start()
        both = dot(v_both, eh)
        outs.append(jnp.transpose((both[:HS] + (both[HS:] + dot(vh, el))) * over))
    o_out[...] = jnp.concatenate(
        [jnp.concatenate(outs[:steps // 2], axis=0), jnp.concatenate(outs[steps // 2:], axis=0)], axis=1
    )
    for c in range(steps):
        here = pl.ds(c * TILE, TILE)
        pltpu.make_async_copy(slopes.at[here], slopes_hbm.at[here], slope_sems.at[c]).wait()
        pltpu.make_async_copy(eh_all.at[c], eh_hbm.at[c], e_sems.at[0, c]).wait()
        pltpu.make_async_copy(el_all.at[c], el_hbm.at[c], e_sems.at[1, c]).wait()


def decode_kernel(
    info, o_parts, x_own, targets_here, targets_there, w_out, w_head,
    log_rate, do_out, dy_out, shared_hbm, yn_all, grads_out, sem,
):
    half = info[0]
    parts = [o_parts[h * OWN:(h + 1) * OWN, :] for h in range(HEADS)]
    attended = jnp.concatenate(
        [jnp.concatenate([p[:, :HS] for p in parts], axis=1), jnp.concatenate([p[:, HS:] for p in parts], axis=1)], axis=0
    )
    wout = w_out[...]
    wouth, woutl = split2(wout)
    ah, al = split2(attended)
    both = dot(jnp.concatenate([ah, al], axis=0), wouth)
    y = x_own[...] + (both[:2 * OWN] + (both[2 * OWN:] + dot(ah, woutl)))
    scale = rms_scale(y)
    yn = y * scale
    yn_all[...] = yn
    rate = dot3_narrow(yn, w_head[...])
    log_rate[...] = rate[:OWN]
    targets = jnp.concatenate([targets_here[...], targets_there[...]], axis=0).astype(F32)
    d_rate = (jnp.exp(rate) - targets) * (1.0 / math.sqrt(TOKENS))
    d_yn = dot3_thin(d_rate, jnp.transpose(w_head[...]))
    dy = scale * (d_yn - yn * jnp.mean(d_yn * yn, axis=-1, keepdims=True))
    dy_out[...] = dy
    dth, dtl = split2(jnp.transpose(dy))
    both = dot(wouth, jnp.concatenate([dth, dtl], axis=1))
    do_out[...] = both[:, :2 * OWN] + (both[:, 2 * OWN:] + dot(woutl, dth))

    heads = o_parts[pl.ds(pl.multiple_of(half * 256, 256), 256), :]
    o_t = jnp.concatenate(
        [
            jnp.concatenate(
                [jnp.transpose(heads[h * OWN:(h + 1) * OWN, :])[:HS], jnp.transpose(heads[h * OWN:(h + 1) * OWN, :])[HS:]], axis=1
            )
            for h in range(4)
        ],
        axis=0,
    )
    d_out = dot3_thin(o_t, dy)
    yn_half = yn_all[:, pl.ds(pl.multiple_of(half * 384, 128), 384)]
    d_head = dot3_thin(jnp.transpose(yn_half), d_rate)
    for p in range(GROUP):
        for j in range(6):
            grads_out[p, 32 * j:32 * j + 32, :] = d_out[32 * p:32 * p + 32, 128 * j:128 * j + 128]
        grads_out[p, 192:240, :] = d_head[48 * p:48 * p + 48, :]
    copy = pltpu.make_async_copy(grads_out, shared_hbm.at[:, 96:336], sem)
    copy.start()
    copy.wait()


def attend_back_kernel(
    info, do_parts, qkv_ref, inverse, w_t, hot_t, scales, dy, eh_hbm, el_hbm, xh_hbm, xl_hbm, slopes_hbm, _,
    shared_hbm,
    sent, eh_all, el_all, xh, xl, slopes, do_all, g_t, dk_acc, dv_acc, dy_all, conv_acc, dconv, sems, e_sems, sent_sem,
):
    half, m = info[0], info[1]
    steps = TOKENS // TILE
    e_copies = [
        [pltpu.make_async_copy(there.at[c], here.at[c], e_sems.at[i, c]) for i, (there, here) in enumerate(((eh_hbm, eh_all), (el_hbm, el_all)))]
        for c in range(steps)
    ]
    copies = [pltpu.make_async_copy(a, b, sems.at[i]) for i, (a, b) in enumerate(((xh_hbm, xh), (xl_hbm, xl), (slopes_hbm, slopes)))]
    for pair in e_copies:
        for copy in pair:
            copy.start()
    for copy in copies:
        copy.start()
    for p in range(GROUP):
        both = jnp.transpose(do_parts[p * OWN:(p + 1) * OWN, :])
        do_all[p * OWN:(p + 1) * OWN, :] = both[:OWN]
        do_all[512 + p * OWN:512 + (p + 1) * OWN, :] = both[OWN:]
    qkv = qkv_ref[...]
    kh, kl = split2(jnp.transpose(qkv[:, HS:2 * HS]))
    k_both = jnp.concatenate([kh, kl], axis=0)
    vh, vl = split2(qkv[:, 2 * HS:])
    v_three = jnp.concatenate([vh, vh, vl], axis=1)
    turned = jnp.transpose(do_all[...])
    dth, dtl = split2(turned)
    do_t = jnp.concatenate([dth, dtl, dth], axis=0)
    dh, dl = split2(jnp.transpose(turned * inverse[...]))
    do_both = jnp.concatenate([dh, dl], axis=1)
    qh, ql = split2(qkv[:, :HS])
    q_both = jnp.concatenate([qh, ql], axis=1)
    dy_all[...] = jnp.zeros_like(dy_all)
    for part in range(2):
        dy_all[pl.ds(pl.multiple_of(part * 512 + m * OWN, OWN), OWN), :] = dy[part * OWN:(part + 1) * OWN, :]
    for c in range(steps):
        here = slice(c * TILE, (c + 1) * TILE)
        dp = dot(v_three, do_t[:, here])
        for copy in e_copies[c]:
            copy.wait()
        eh, el = eh_all[c], el_all[c]
        p = (eh.astype(F32) + el.astype(F32)) * inverse[:, here]
        ds = p * (dp - jnp.sum(p * dp, axis=0, keepdims=True))
        sh, sl = split2(ds)
        both = dot(k_both, sh)
        g_t[0:HS, here] = (both[:HS] + (both[HS:] + dot(kh, sl))) * (HS ** -0.5)
        both = dot(eh, do_both[here])
        dv = both[:, :HS] + (both[:, HS:] + dot(el, dh[here]))
        both = dot(sh, q_both[here])
        dk = both[:, :HS] + (both[:, HS:] + dot(sl, qh[here]))
        if c == 0:
            dk_acc[...] = dk
            dv_acc[...] = dv
        else:
            dk_acc[...] += dk
            dv_acc[...] += dv
    g_t[HS:2 * HS, :] = jnp.transpose(dk_acc[...])
    g_t[2 * HS:3 * HS, :] = jnp.transpose(dv_acc[...])
    for copy in copies:
        copy.wait()
    lanes = pl.ds(pl.multiple_of(half * 384, 128), 384)
    gh, gl = split2(g_t[...])
    both = dot(jnp.concatenate([gh, gl], axis=0), xh[:, lanes])
    d_w = jnp.transpose(both[:192] + (both[192:] + dot(gh, xl[:, lanes])))

    wh, wl = split2(w_t[...])
    w_three = jnp.concatenate([wh, wl, wh], axis=0)
    for c in range(steps):
        here = slice(c * TILE, (c + 1) * TILE)
        gh, gl = split2(jnp.transpose(g_t[:, here]))
        d_xn = dot(jnp.concatenate([gh, gh, gl], axis=1), w_three)
        xn = xh[here].astype(F32) + xl[here].astype(F32)
        mean = jnp.mean(d_xn * xn, axis=-1, keepdims=True)
        d_x = (dy_all[here] + scales[here, :1] * (d_xn - xn * mean)) * (1.0 / POOL)
        hot = hot_t[:, here]
        hot_two = jnp.concatenate([hot, hot], axis=1)
        for r in range(POOL):
            dh, dl = split2(d_x * slopes[here, r * C:(r + 1) * C])
            moved = dot(hot_two, jnp.concatenate([dh, dl], axis=0))
            if c == 0:
                conv_acc[r] = moved
            else:
                conv_acc[r] += moved
    summed = conv_acc[0, 4:4 + 4 * KW, :]
    for r in range(1, POOL):
        summed += conv_acc[r, 4 * (r + 1):4 * (r + 1) + 4 * KW, :]
    dconv[...] = jnp.zeros_like(dconv)
    dconv[0:4 * KW, :] = summed
    d_conv = jnp.transpose(dconv[:, lanes])
    for p in range(GROUP):
        mine = d_w[48 * p:48 * p + 48, :]
        sent[p, 0:48, :] = mine[:, :128]
        sent[p, 48:72, :] = jnp.concatenate([mine[:24, 128:], mine[24:, 128:]], axis=1)
        mine = d_conv[48 * p:48 * p + 48, :HS]
        sent[p, 72:96, :] = jnp.concatenate([mine[:24], mine[24:]], axis=1)
    copy = pltpu.make_async_copy(sent, shared_hbm.at[:, 0:96], sent_sem)
    copy.start()
    copy.wait()


def finish_kernel(got, d_conv, d_query, d_key, d_value, d_out, d_head):
    total = got[0, 72:96, :]
    every = got[0, 96:336, :]
    for p in range(1, GROUP):
        total = total + got[p, 72:96, :]
        every = every + got[p, 96:336, :]
    d_conv[...] = jnp.concatenate([total[:, :HS], total[:, HS:]], axis=0)[:, :4 * KW]
    d_out[...] = jnp.concatenate([every[32 * j:32 * j + 32, :] for j in range(6)], axis=1)
    d_head[...] = every[192:240, :]
    for part, out in enumerate((d_query, d_key)):
        out[...] = jnp.concatenate([got[h, 0:48, part * HS:(part + 1) * HS] for h in range(HEADS)], axis=1)
    rows = [got[h, 48:72, :] for h in range(HEADS)]
    d_value[...] = jnp.concatenate([jnp.concatenate([r[:, :HS], r[:, HS:]], axis=0) for r in rows], axis=1)


def shape(*dims, dtype=F32):
    return jax.ShapeDtypeStruct(dims, dtype)


def params(mib=60):
    return pltpu.CompilerParams(vmem_limit_bytes=mib * 1024 * 1024)


def per_device(bases, targets, w_conv, w_query, w_key, w_value, w_out, w_head):
    s = lax.axis_index("seq")
    info = jnp.stack([lax.div(s, GROUP), lax.rem(s, GROUP)]).astype(jnp.int32)
    groups = [list(range(GROUP)), list(range(GROUP, 2 * GROUP))]

    def exchange(value):
        return lax.all_to_all(value, "seq", 0, 0, axis_index_groups=groups, tiled=True)

    targets_there = lax.ppermute(targets, "seq", [(i, i ^ GROUP) for i in range(2 * GROUP)])
    every = lax.all_to_all(jnp.broadcast_to(bases.reshape(1, 2, 128), (16, 2, 128)), "seq", 0, 0, tiled=True)

    xh, xl, scales, x_own, hot_t, qkv, w_t, inverse, o_here, slopes, eh, el = pl.pallas_call(
        attend_kernel,
        out_shape=(
            shape(TOKENS, C, dtype=BF16), shape(TOKENS, C, dtype=BF16), shape(TOKENS, 128), shape(2 * OWN, C),
            shape(128, TOKENS, dtype=BF16), shape(TOKENS, 3 * HS), shape(3 * HS, C), shape(1, TOKENS), shape(512, 128),
            shape(TOKENS, POOL * C), shape(4, TOKENS, TILE, dtype=BF16), shape(4, TOKENS, TILE, dtype=BF16),
        ),
        in_specs=[SMEM, VMEM, VMEM, ANY, ANY, ANY],
        out_specs=(VMEM,) * 9 + (ANY,) * 3,
        scratch_shapes=[
            pltpu.VMEM((POOL, WIN, C), F32),
            pltpu.VMEM((256, POOL * C), BF16),
            pltpu.VMEM((TOKENS + 16, 256), F32),
            pltpu.VMEM((3, C, 128), F32),
            pltpu.VMEM((TOKENS, C), F32),
            pltpu.VMEM((TOKENS, POOL * C), F32),
            pltpu.VMEM((4, TOKENS, TILE), BF16),
            pltpu.VMEM((4, TOKENS, TILE), BF16),
            pltpu.SemaphoreType.DMA((3,)),
            pltpu.SemaphoreType.DMA((4,)),
            pltpu.SemaphoreType.DMA((2, 4)),
        ],
        compiler_params=params(),
        name="attend",
    )(info, every, w_conv, w_query, w_key, w_value)

    log_rate, do_sent, dy, shared = pl.pallas_call(
        decode_kernel,
        out_shape=(shape(OWN, TRACKS), shape(HD, 128), shape(2 * OWN, C), shape(GROUP, 336, 128)),
        in_specs=[SMEM] + [VMEM] * 6,
        out_specs=(VMEM,) * 3 + (ANY,),
        scratch_shapes=[pltpu.VMEM((2 * OWN, C), F32), pltpu.VMEM((GROUP, 240, 128), F32), pltpu.SemaphoreType.DMA],
        compiler_params=params(),
        name="decode",
    )(info, exchange(o_here), x_own, targets, targets_there, w_out, w_head)

    sent = pl.pallas_call(
        attend_back_kernel,
        out_shape=shape(GROUP, 336, 128),
        in_specs=[SMEM] + [VMEM] * 7 + [ANY] * 6,
        out_specs=ANY,
        input_output_aliases={13: 0},
        scratch_shapes=[
            pltpu.VMEM((GROUP, 96, 128), F32),
            pltpu.VMEM((4, TOKENS, TILE), BF16),
            pltpu.VMEM((4, TOKENS, TILE), BF16),
            pltpu.VMEM((TOKENS, C), BF16),
            pltpu.VMEM((TOKENS, C), BF16),
            pltpu.VMEM((TOKENS, POOL * C), F32),
            pltpu.VMEM((TOKENS, HS), F32),
            pltpu.VMEM((3 * HS, TOKENS), F32),
            pltpu.VMEM((TOKENS, HS), F32),
            pltpu.VMEM((TOKENS, HS), F32),
            pltpu.VMEM((TOKENS, C), F32),
            pltpu.VMEM((POOL, 128, C), F32),
            pltpu.VMEM((128, C), F32),
            pltpu.SemaphoreType.DMA((3,)),
            pltpu.SemaphoreType.DMA((2, 4)),
            pltpu.SemaphoreType.DMA,
        ],
        compiler_params=params(),
        name="attend_back",
    )(info, exchange(do_sent), qkv, inverse, w_t, hot_t, scales, dy, eh, el, xh, xl, slopes, shared)

    d_conv, d_query, d_key, d_value, d_out, d_head = pl.pallas_call(
        finish_kernel,
        out_shape=(shape(48, 4 * KW), shape(48, HD), shape(48, HD), shape(48, HD), shape(32, C), shape(48, TRACKS)),
        in_specs=[VMEM],
        out_specs=(VMEM,) * 6,
        compiler_params=params(),
        name="finish",
    )(exchange(sent))
    return (log_rate, jnp.transpose(d_conv), d_query, d_key, d_value, d_out, d_head)


def solution(mesh):
    rows = P(("dp", "seq"), None)
    return jax.shard_map(
        per_device,
        mesh=mesh,
        in_specs=(P(("dp", "seq")), rows, P(), P(), P(), P(), P(), P()),
        out_specs=(rows, P("dp", "seq"), rows, rows, rows, rows, rows),
        check_vma=False,
    )
```

time: 151 us -> 110 us (0.73)
  waiting for transfers between devices: 45 us -> 14 us
  blocking collectives: 11 us -> 31.4 us
  local copies, waits for them, and re-layouts: 22.8 us -> 2.64 us
  between operations: 14.2 us -> 0.69 us
  Pallas kernels: 34.3 us -> 47.2 us
  starting transfers between devices: 21.5 us -> 12.5 us
    all_to_all x1 -> x2, blocking collectives: 11 us -> 31.4 us  [exchange(): lax.all_to_all(value, 'seq', 0, 0, axis_index_groups=groups, tiled=True)]
    reduce_scatter x1 -> x0, waiting for transfers between devices: 20.3 us -> none  [per_device(): lax.psum_scatter(grads_part, 'seq', scatter_dimension=0, axis_index_group...]
    unnamed x59 -> x8, local copies, waits for them, and re-layouts: 21.5 us -> 1.35 us
    all_to_all x3 -> x1, waiting for transfers between devices: 12.2 us -> 2.14 us  [exchange(): lax.all_to_all(value, 'seq', 0, 0, axis_index_groups=groups, tiled=True)]
    all_to_all x3 -> x1, starting transfers between devices: 12.2 us -> 3.42 us  [exchange(): lax.all_to_all(value, 'seq', 0, 0, axis_index_groups=groups, tiled=True)]
    pallas_call x1, Pallas kernels: 15 us -> 22.3 us  [per_device(): pl.pallas_call(attend_kernel, out_shape=(shape(TOKENS, C, dtype=BF16), sh...]
    pallas_call x3 -> x2, Pallas kernels: 16 us -> 19.1 us  [the longest x1 16.9 us: per_device(): pl.pallas_call(attend_back_kernel, out_shape=shape(GROUP, 336, 128), in_s...]
    pallas_call x1, Pallas kernels: 3.39 us -> 5.81 us  [per_device(): pl.pallas_call(decode_kernel, out_shape=(shape(OWN, TRACKS), shape(HD, 12...]
  transfers between devices with their start and end apart: 6 -> 3, of which waited for: 5 -> 3; matrix products, arithmetic and copies ran while one was open for 0% -> 1% of each run, Pallas kernels for 3% -> 0%
where the time goes in v2:
time: 110 us; the launch traced here: 109 us
  Pallas kernels  47.2 us (43%)
  blocking collectives  31.4 us (29%)
  waiting for transfers between devices  14 us (13%)
  starting transfers between devices  12.5 us (11%)
  local copies, waits for them, and re-layouts  2.64 us (2%)
    all_to_all x2, blocking collectives, exchange(): lax.all_to_all(value, 'seq', 0, 0, axis_index_groups=groups, tiled=True)  31.4 us
    pallas_call x1, Pallas kernels, per_device(): pl.pallas_call(attend_kernel, out_shape=(shape(TOKENS, C, dtype=BF16), sh...  22.3 us
    pallas_call x1, Pallas kernels, per_device(): pl.pallas_call(attend_back_kernel, out_shape=shape(GROUP, 336, 128), in_s...  16.9 us
    all_to_all x1, starting transfers between devices, per_device(): lax.all_to_all(jnp.broadcast_to(bases.reshape(1, 2, 128), (16, 2, 128)),...  8.47 us
    all_to_all x1, waiting for transfers between devices, per_device(): lax.all_to_all(jnp.broadcast_to(bases.reshape(1, 2, 128), (16, 2, 128)),...  7.41 us
    pallas_call x1, Pallas kernels, per_device(): pl.pallas_call(decode_kernel, out_shape=(shape(OWN, TRACKS), shape(HD, 12...  5.81 us
    ppermute x1, waiting for transfers between devices, per_device(): lax.ppermute(targets, 'seq', [(i, i ^ GROUP) for i in range(2 * GROUP)])  4.44 us
    all_to_all x1, starting transfers between devices, exchange(): lax.all_to_all(value, 'seq', 0, 0, axis_index_groups=groups, tiled=True)  3.42 us
  transfers between devices with their start and end apart: 3, of which 3 were waited for; matrix products, arithmetic and copies ran while one was open for 1% of the time, Pallas kernels for 0%

profile of v2, /device:TPU:16, one launch (start us, length us, event | category | flops | bytes accessed | tf_op | source)
XLA Modules:
  0.0 109.0 jit_solution(14238666904823757589)
XLA Ops:
  0.6 1.3 %broadcast_in_dim.8 = s32[16,2,128]{2,1,0:T(2,128)} broadcast(s32[2,128]{1,0:T(2,128)} %bitcast.12), dimensions={1,2} | broadcast | bytes 17408 | tf_op jit(solution)/shard_map/broadcast_in_dim | solution.py:400
  1.9 8.5 %all-to-all-start = ((s32[16,2,128]{2,1,0:T(2,128)}), s32[16,2,128]{2,1,0:T(2,128)S(1)}, u32[]{:S(2)}, u32[]{:S(2)}) async-start(s32[16,2,128]{2,1,0:T(2,128)} %broadcast_in_dim.8), calls=%async_computation | async-start | bytes 32768 | tf_op jit(solution)/shard_map/all_to_all | solution.py:400
  10.4 0.6 pad_add_fusion.info
  11.0 0.0 copy-start.2
  11.0 7.4 %all-to-all-done.bases = s32[16,2,128]{2,1,0:T(2,128)S(1)} async-done(((s32[16,2,128]{2,1,0:T(2,128)}), s32[16,2,128]{2,1,0:T(2,128)S(1)}, u32[]{:S(2)}, u32[]{:S(2)}) %all-to-all-start) | async-done | bytes 16416 | tf_op jit(solution)/shard_map/all_to_all | solution.py:400
  18.4 0.0 copy-start.1
  18.4 0.6 copy-done.1
  19.0 22.3 %attend.1 = (bf16[1024,768]{1,0:T(8,128)(2,1)}, bf16[1024,768]{1,0:T(8,128)(2,1)}, f32[1024,128]{1,0:T(8,128)}, f32[128,768]{1,0:T(8,128)}, bf16[128,1024]{1,0:T...) custom-call(s32[2]{0:T(128)} %pad_add_fusion.info, ...), custom_call_target="tpu_custom_call" | custom-call | tf_op jit(solution)/shard_map/attend/pallas_call | solution.py:402
  41.4 3.4 %all-to-all-start.1 = ((f32[8,64,128]{2,1,0:T(8,128)}), f32[8,64,128]{2,1,0:T(8,128)S(1)}, u32[]{:S(2)}, u32[]{:S(2)}) async-start(f32[8,64,128]{2,1,0:T(8,128)} %bitcast.10), calls=%async_computation.1 | async-start | bytes 524288 | tf_op jit(solution)/shard_map/all_to_all | solution.py:397
  44.8 0.0 copy-done.2
  44.8 0.6 collective-permute-start
  45.4 4.4 %collective-permute-done.targets_there = s32[64,128]{1,0:T(8,128)S(1)} collective-permute-done((s32[64,128]{1,0:T(8,128)S(1)}, s32[64,128]{1,0:T(8,128)S(1)}, u32[]{:S(2)}, u32[]{:S(2)}) %collective-permute-start) | collective-permute-done | bytes 32800 | tf_op jit(solution)/shard_map/ppermute | solution.py:399
  49.8 0.0 copy-start.3
  49.8 2.1 %all-to-all-done.1 = f32[8,64,128]{2,1,0:T(8,128)S(1)} async-done(((f32[8,64,128]{2,1,0:T(8,128)}), f32[8,64,128]{2,1,0:T(8,128)S(1)}, u32[]{:S(2)}, u32[]{:S(2)}) %all-to-all-start.1) | async-done | bytes 262176 | tf_op jit(solution)/shard_map/all_to_all | solution.py:397
  51.9 0.0 copy-start
  51.9 0.0 copy-done.3
  51.9 0.7 copy-done
  52.7 5.8 %decode.1 = (f32[64,128]{1,0:T(8,128)}, f32[512,128]{1,0:T(8,128)}, f32[128,768]{1,0:T(8,128)}, f32[8,336,128]{2,1,0:T(8,128)}) custom-call(s32[2]{0:T(128)} %pad_add_fusion.info, f32[512,128]{1,0:T(8,128)} %bitcast.9, f32[128,768]{1,0:T(8,128)} %get-tuple-element.30.x_own, s32[64,128]{1,0:T(8,128)} %targets_here.1, s32[64,128]{1,0:T(8,128)} %copy-done.3, ...), custom_call_target="tpu_custom_call" | custom-call | tf_op jit(solution)/shard_map/decode/pallas_call | solution.py:428
  58.5 11.3 %all_to_all.32 = f32[8,64,128]{2,1,0:T(8,128)} all-to-all(f32[8,64,128]{2,1,0:T(8,128)} %bitcast.11), channel_id=1, replica_groups={{0,16,32,48,64,80,96,112},{128,144,160,176,192,208,224,240},{1,17,33,49..., dimensions={0} | all-to-all | bytes 524288 | tf_op jit(solution)/shard_map/all_to_all | solution.py:397
  69.8 16.9 %attend_back.1 = f32[8,336,128]{2,1,0:T(8,128)} custom-call(s32[2]{0:T(128)} %pad_add_fusion.info, f32[512,128]{1,0:T(8,128)} %bitcast.8, f32[1024,192]{1,0:T(8,128)} %get-tuple-element.33.qkv_ref, f32[1,1024]{1,0:T(1,128)} %get-tuple-element.34.inverse, f32[192,768]{1,0:T(8,128)} %get-tuple-element.35.w_t, ...), custom_call_target="tpu_custom_call", output_to_operand_aliasing={{}: (13, {})} | custom-call | tf_op jit(solution)/shard_map/attend_back/pallas_call | solution.py:438
  86.6 20.2 %all_to_all.33.got = f32[8,336,128]{2,1,0:T(8,128)} all-to-all(f32[8,336,128]{2,1,0:T(8,128)} %attend_back.1), channel_id=1, replica_groups={{0,16,32,48,64,80,96,112},{128,144,160,176,192,208,224,240},{1,17,33,49..., dimensions={0} | all-to-all | bytes 2752512 | tf_op jit(solution)/shard_map/all_to_all | solution.py:397
  106.8 2.2 %finish.1 = (f32[48,60]{1,0:T(8,128)}, f32[48,512]{1,0:T(8,128)}, f32[48,512]{1,0:T(8,128)}, f32[48,512]{1,0:T(8,128)}, f32[32,768]{1,0:T(8,128)}, /*index=5*/f32[48,128]{1,0:T(8,128)}) custom-call(f32[8,336,128]{2,1,0:T(8,128)} %all_to_all.33.got), custom_call_target="tpu_custom_call" | custom-call | tf_op jit(solution)/shard_map/finish/pallas_call | solution.py:466
Async XLA Ops:
  1.9 16.5 %all-to-all-start = ((s32[16,2,128]{2,1,0:T(2,128)}), s32[16,2,128]{2,1,0:T(2,128)S(1)}, u32[]{:S(2)}, u32[]{:S(2)}) async-start(s32[16,2,128]{2,1,0:T(2,128)} %broadcast_in_dim.8), calls=%async_computation | async-start | bytes 32768 | tf_op jit(solution)/shard_map/all_to_all | solution.py:400
  11.0 33.8 %copy-start.2 = (s32[64,128]{1,0:T(8,128)S(1)}, s32[64,128]{1,0:T(8,128)}, u32[]{:S(2)}) copy-start(s32[64,128]{1,0:T(8,128)} %targets_here.1) | copy-start | bytes 98308
  18.4 0.6 copy-start.1
  41.4 10.6 %all-to-all-start.1 = ((f32[8,64,128]{2,1,0:T(8,128)}), f32[8,64,128]{2,1,0:T(8,128)S(1)}, u32[]{:S(2)}, u32[]{:S(2)}) async-start(f32[8,64,128]{2,1,0:T(8,128)} %bitcast.10), calls=%async_computation.1 | async-start | bytes 524288 | tf_op jit(solution)/shard_map/all_to_all | solution.py:397
  44.8 5.0 %collective-permute-start = (s32[64,128]{1,0:T(8,128)S(1)}, s32[64,128]{1,0:T(8,128)S(1)}, u32[]{:S(2)}, u32[]{:S(2)}) collective-permute-start(s32[64,128]{1,0:T(8,128)S(1)} %copy-done.2), channel_id=1, source_target_pairs={{0,128},{16,144},{32,160},{48,176},{64,192},{80,208},{96,224},{112... | collective-permute-start | bytes 98312 | tf_op jit(solution)/shard_map/ppermute | solution.py:399
  49.8 2.1 %copy-start.3 = (s32[64,128]{1,0:T(8,128)}, s32[64,128]{1,0:T(8,128)S(1)}, u32[]{:S(2)}) copy-start(s32[64,128]{1,0:T(8,128)S(1)} %collective-permute-done.targets_there) | copy-start | bytes 98308
  51.9 0.7 copy-start

commit v3 on v2

--- a/solution.py
+++ b/solution.py
@@ -21,7 +21,7 @@
 F32 = jnp.float32
 BF16 = jnp.bfloat16
 GELU_A = math.sqrt(2.0 / math.pi)
-GELU_B = GELU_A * 0.044715
+GELU_C = 0.044715 / GELU_A ** 2
 WIN = 80
 TILE = 256
 
@@ -87,7 +87,7 @@
 def conv_weights(w_ref, pad_ref, out_ref):
     pad_ref[...] = jnp.zeros_like(pad_ref)
     for r in range(POOL):
-        pad_ref[r, 4 * (r + 1):4 * (r + 1) + 4 * KW, :] = w_ref[...]
+        pad_ref[r, 4 * (r + 1):4 * (r + 1) + 4 * KW, :] = w_ref[...] * GELU_A
     for r in range(POOL):
         pieces = split3(pad_ref[r])
         zeros = jnp.zeros((256 - 3 * WIN, C), BF16)
@@ -106,8 +106,8 @@
 
 def attend_kernel(
     info, bases, w_conv, wq_hbm, wk_hbm, wv_hbm,
-    xh_out, xl_out, scale_out, x_own, hot_t, qkv_out, w_t, inverse, o_out, slopes_hbm, eh_hbm, el_hbm,
-    pad, w_all, window, slabs, x_all, slopes, eh_all, el_all, sems, slope_sems, e_sems,
+    x_own, hot_t, inverse, o_out, xh_hbm, xl_hbm, scale_hbm, qkv_hbm, w_t_hbm, slopes_hbm, eh_hbm, el_hbm,
+    pad, w_all, window, slabs, x_all, xh_out, xl_out, scale_out, qkv_out, w_t, slopes, eh_all, el_all, sems, slope_sems, e_sems, out_sems,
 ):
     half, m = info[0], info[1]
     copies = []
@@ -147,15 +147,15 @@
             hot = jnp.where(shift == d, around[6 + d:6 + d + TILE, :], hot)
         hot = jnp.where(real, hot, 0.0).astype(BF16)
         here = pl.ds(pl.multiple_of(c * TILE, TILE), TILE)
-        total = jnp.zeros((TILE, C), F32)
+        total = None
         for r in range(POOL):
-            pre = dot(hot, w_all[:, r * C:(r + 1) * C])
-            square = pre * pre
-            t = jnp.tanh(pre * (GELU_A + GELU_B * square))
-            near = 0.5 + 0.5 * t
-            total += pre * near
-            slopes[here, r * C:(r + 1) * C] = near + pre * (near * (1.0 - t)) * (GELU_A + 3.0 * GELU_B * square)
-        x_all[here, :] = total * (1.0 / POOL)
+            y = dot(hot, w_all[:, r * C:(r + 1) * C])
+            b = y * y * GELU_C
+            t = jnp.tanh(y + y * b)
+            up = 1.0 + t
+            total = y * up if total is None else total + y * up
+            slopes[here, r * C:(r + 1) * C] = up + (1.0 - t * t) * (y + y * (3.0 * b))
+        x_all[here, :] = total * (0.5 / (GELU_A * POOL))
         hot_t[:, here] = jnp.transpose(hot[:, :128].astype(F32)).astype(BF16)
         pltpu.make_async_copy(slopes.at[here], slopes_hbm.at[here], slope_sems.at[c]).start()
         return 0
@@ -186,6 +186,12 @@
         here = pl.ds(pl.multiple_of(part * 512 + m * OWN, OWN), OWN)
         x_own[part * OWN:(part + 1) * OWN, :] = x_all[here, :]
 
+    outs_copies = [
+        pltpu.make_async_copy(a, b, out_sems.at[i])
+        for i, (a, b) in enumerate(((xh_out, xh_hbm), (xl_out, xl_hbm), (scale_out, scale_hbm), (qkv_out, qkv_hbm), (w_t, w_t_hbm)))
+    ]
+    for copy in outs_copies:
+        copy.start()
     qkv = qkv_out[...]
     q_t = query_stack(jnp.transpose(qkv[:, :HS]))
     keys = key_stack(qkv[:, HS:2 * HS])
@@ -207,6 +213,8 @@
     o_out[...] = jnp.concatenate(
         [jnp.concatenate(outs[:steps // 2], axis=0), jnp.concatenate(outs[steps // 2:], axis=0)], axis=1
     )
+    for copy in outs_copies:
+        copy.wait()
     for c in range(steps):
         here = pl.ds(c * TILE, TILE)
         pltpu.make_async_copy(slopes.at[here], slopes_hbm.at[here], slope_sems.at[c]).wait()
@@ -216,7 +224,7 @@
 
 def decode_kernel(
     info, o_parts, x_own, targets_here, targets_there, w_out, w_head,
-    log_rate, do_out, dy_out, shared_hbm, yn_all, grads_out, sem,
+    log_rate, do_out, dy_out, grads_hbm, yn_all, grads_out, sem,
 ):
     half = info[0]
     parts = [o_parts[h * OWN:(h + 1) * OWN, :] for h in range(HEADS)]
@@ -238,10 +246,6 @@
     d_yn = dot3_thin(d_rate, jnp.transpose(w_head[...]))
     dy = scale * (d_yn - yn * jnp.mean(d_yn * yn, axis=-1, keepdims=True))
     dy_out[...] = dy
-    dth, dtl = split2(jnp.transpose(dy))
-    both = dot(wouth, jnp.concatenate([dth, dtl], axis=1))
-    do_out[...] = both[:, :2 * OWN] + (both[:, 2 * OWN:] + dot(woutl, dth))
-
     heads = o_parts[pl.ds(pl.multiple_of(half * 256, 256), 256), :]
     o_t = jnp.concatenate(
         [
@@ -259,15 +263,18 @@
         for j in range(6):
             grads_out[p, 32 * j:32 * j + 32, :] = d_out[32 * p:32 * p + 32, 128 * j:128 * j + 128]
         grads_out[p, 192:240, :] = d_head[48 * p:48 * p + 48, :]
-    copy = pltpu.make_async_copy(grads_out, shared_hbm.at[:, 96:336], sem)
+    copy = pltpu.make_async_copy(grads_out, grads_hbm, sem)
     copy.start()
+    dth, dtl = split2(jnp.transpose(dy))
+    both = dot(wouth, jnp.concatenate([dth, dtl], axis=1))
+    do_out[...] = both[:, :2 * OWN] + (both[:, 2 * OWN:] + dot(woutl, dth))
     copy.wait()
 
 
 def attend_back_kernel(
-    info, do_parts, qkv_ref, inverse, w_t, hot_t, scales, dy, eh_hbm, el_hbm, xh_hbm, xl_hbm, slopes_hbm, _,
-    shared_hbm,
-    sent, eh_all, el_all, xh, xl, slopes, do_all, g_t, dk_acc, dv_acc, dy_all, conv_acc, dconv, sems, e_sems, sent_sem,
+    info, do_parts, qkv_ref, inverse, w_t, hot_t, scales, dy, eh_hbm, el_hbm, xh_hbm, xl_hbm, slopes_hbm,
+    sent,
+    eh_all, el_all, xh, xl, slopes, do_all, g_t, dk_acc, dv_acc, dy_all, conv_acc, dconv, sems, e_sems,
 ):
     half, m = info[0], info[1]
     steps = TOKENS // TILE
@@ -275,7 +282,10 @@
         [pltpu.make_async_copy(there.at[c], here.at[c], e_sems.at[i, c]) for i, (there, here) in enumerate(((eh_hbm, eh_all), (el_hbm, el_all)))]
         for c in range(steps)
     ]
-    copies = [pltpu.make_async_copy(a, b, sems.at[i]) for i, (a, b) in enumerate(((xh_hbm, xh), (xl_hbm, xl), (slopes_hbm, slopes)))]
+    copies = [pltpu.make_async_copy(a, b, sems.at[i]) for i, (a, b) in enumerate(((xh_hbm, xh), (xl_hbm, xl)))]
+    copies += [
+        pltpu.make_async_copy(slopes_hbm.at[pl.ds(c * TILE, TILE)], slopes.at[pl.ds(c * TILE, TILE)], sems.at[2 + c]) for c in range(steps)
+    ]
     for pair in e_copies:
         for copy in pair:
             copy.start()
@@ -323,8 +333,8 @@
             dv_acc[...] += dv
     g_t[HS:2 * HS, :] = jnp.transpose(dk_acc[...])
     g_t[2 * HS:3 * HS, :] = jnp.transpose(dv_acc[...])
-    for copy in copies:
-        copy.wait()
+    copies[0].wait()
+    copies[1].wait()
     lanes = pl.ds(pl.multiple_of(half * 384, 128), 384)
     gh, gl = split2(g_t[...])
     both = dot(jnp.concatenate([gh, gl], axis=0), xh[:, lanes])
@@ -338,7 +348,8 @@
         d_xn = dot(jnp.concatenate([gh, gh, gl], axis=1), w_three)
         xn = xh[here].astype(F32) + xl[here].astype(F32)
         mean = jnp.mean(d_xn * xn, axis=-1, keepdims=True)
-        d_x = (dy_all[here] + scales[here, :1] * (d_xn - xn * mean)) * (1.0 / POOL)
+        d_x = (dy_all[here] + scales[here, :1] * (d_xn - xn * mean)) * (0.5 / POOL)
+        copies[2 + c].wait()
         hot = hot_t[:, here]
         hot_two = jnp.concatenate([hot, hot], axis=1)
         for r in range(POOL):
@@ -360,17 +371,14 @@
         sent[p, 48:72, :] = jnp.concatenate([mine[:24, 128:], mine[24:, 128:]], axis=1)
         mine = d_conv[48 * p:48 * p + 48, :HS]
         sent[p, 72:96, :] = jnp.concatenate([mine[:24], mine[24:]], axis=1)
-    copy = pltpu.make_async_copy(sent, shared_hbm.at[:, 0:96], sent_sem)
-    copy.start()
-    copy.wait()
-
-
-def finish_kernel(got, d_conv, d_query, d_key, d_value, d_out, d_head):
+
+
+def finish_kernel(got, grads, d_conv, d_query, d_key, d_value, d_out, d_head):
     total = got[0, 72:96, :]
-    every = got[0, 96:336, :]
+    every = grads[0]
     for p in range(1, GROUP):
         total = total + got[p, 72:96, :]
-        every = every + got[p, 96:336, :]
+        every = every + grads[p]
     d_conv[...] = jnp.concatenate([total[:, :HS], total[:, HS:]], axis=0)[:, :4 * KW]
     d_out[...] = jnp.concatenate([every[32 * j:32 * j + 32, :] for j in range(6)], axis=1)
     d_head[...] = every[192:240, :]
@@ -388,61 +396,59 @@
     return pltpu.CompilerParams(vmem_limit_bytes=mib * 1024 * 1024)
 
 
-def per_device(bases, targets, w_conv, w_query, w_key, w_value, w_out, w_head):
-    s = lax.axis_index("seq")
-    info = jnp.stack([lax.div(s, GROUP), lax.rem(s, GROUP)]).astype(jnp.int32)
-    groups = [list(range(GROUP)), list(range(GROUP, 2 * GROUP))]
-
-    def exchange(value):
-        return lax.all_to_all(value, "seq", 0, 0, axis_index_groups=groups, tiled=True)
-
-    targets_there = lax.ppermute(targets, "seq", [(i, i ^ GROUP) for i in range(2 * GROUP)])
-    every = lax.all_to_all(jnp.broadcast_to(bases.reshape(1, 2, 128), (16, 2, 128)), "seq", 0, 0, tiled=True)
-
-    xh, xl, scales, x_own, hot_t, qkv, w_t, inverse, o_here, slopes, eh, el = pl.pallas_call(
+def attend():
+    return pl.pallas_call(
         attend_kernel,
         out_shape=(
-            shape(TOKENS, C, dtype=BF16), shape(TOKENS, C, dtype=BF16), shape(TOKENS, 128), shape(2 * OWN, C),
-            shape(128, TOKENS, dtype=BF16), shape(TOKENS, 3 * HS), shape(3 * HS, C), shape(1, TOKENS), shape(512, 128),
+            shape(2 * OWN, C), shape(128, TOKENS, dtype=BF16), shape(1, TOKENS), shape(512, 128),
+            shape(TOKENS, C, dtype=BF16), shape(TOKENS, C, dtype=BF16), shape(TOKENS, 128), shape(TOKENS, 3 * HS), shape(3 * HS, C),
             shape(TOKENS, POOL * C), shape(4, TOKENS, TILE, dtype=BF16), shape(4, TOKENS, TILE, dtype=BF16),
         ),
         in_specs=[SMEM, VMEM, VMEM, ANY, ANY, ANY],
-        out_specs=(VMEM,) * 9 + (ANY,) * 3,
+        out_specs=(VMEM,) * 4 + (ANY,) * 8,
         scratch_shapes=[
             pltpu.VMEM((POOL, WIN, C), F32),
             pltpu.VMEM((256, POOL * C), BF16),
             pltpu.VMEM((TOKENS + 16, 256), F32),
             pltpu.VMEM((3, C, 128), F32),
             pltpu.VMEM((TOKENS, C), F32),
+            pltpu.VMEM((TOKENS, C), BF16),
+            pltpu.VMEM((TOKENS, C), BF16),
+            pltpu.VMEM((TOKENS, 128), F32),
+            pltpu.VMEM((TOKENS, 3 * HS), F32),
+            pltpu.VMEM((3 * HS, C), F32),
             pltpu.VMEM((TOKENS, POOL * C), F32),
             pltpu.VMEM((4, TOKENS, TILE), BF16),
             pltpu.VMEM((4, TOKENS, TILE), BF16),
             pltpu.SemaphoreType.DMA((3,)),
             pltpu.SemaphoreType.DMA((4,)),
             pltpu.SemaphoreType.DMA((2, 4)),
+            pltpu.SemaphoreType.DMA((5,)),
         ],
         compiler_params=params(),
         name="attend",
-    )(info, every, w_conv, w_query, w_key, w_value)
-
-    log_rate, do_sent, dy, shared = pl.pallas_call(
+    )
+
+
+def decode():
+    return pl.pallas_call(
         decode_kernel,
-        out_shape=(shape(OWN, TRACKS), shape(HD, 128), shape(2 * OWN, C), shape(GROUP, 336, 128)),
+        out_shape=(shape(OWN, TRACKS), shape(HD, 128), shape(2 * OWN, C), shape(GROUP, 240, 128)),
         in_specs=[SMEM] + [VMEM] * 6,
         out_specs=(VMEM,) * 3 + (ANY,),
         scratch_shapes=[pltpu.VMEM((2 * OWN, C), F32), pltpu.VMEM((GROUP, 240, 128), F32), pltpu.SemaphoreType.DMA],
         compiler_params=params(),
         name="decode",
-    )(info, exchange(o_here), x_own, targets, targets_there, w_out, w_head)
-
-    sent = pl.pallas_call(
+    )
+
+
+def attend_back():
+    return pl.pallas_call(
         attend_back_kernel,
-        out_shape=shape(GROUP, 336, 128),
-        in_specs=[SMEM] + [VMEM] * 7 + [ANY] * 6,
-        out_specs=ANY,
-        input_output_aliases={13: 0},
+        out_shape=shape(GROUP, 96, 128),
+        in_specs=[SMEM] + [VMEM] * 7 + [ANY] * 5,
+        out_specs=VMEM,
         scratch_shapes=[
-            pltpu.VMEM((GROUP, 96, 128), F32),
             pltpu.VMEM((4, TOKENS, TILE), BF16),
             pltpu.VMEM((4, TOKENS, TILE), BF16),
             pltpu.VMEM((TOKENS, C), BF16),
@@ -455,22 +461,42 @@
             pltpu.VMEM((TOKENS, C), F32),
             pltpu.VMEM((POOL, 128, C), F32),
             pltpu.VMEM((128, C), F32),
-            pltpu.SemaphoreType.DMA((3,)),
+            pltpu.SemaphoreType.DMA((6,)),
             pltpu.SemaphoreType.DMA((2, 4)),
-            pltpu.SemaphoreType.DMA,
         ],
         compiler_params=params(),
         name="attend_back",
-    )(info, exchange(do_sent), qkv, inverse, w_t, hot_t, scales, dy, eh, el, xh, xl, slopes, shared)
-
-    d_conv, d_query, d_key, d_value, d_out, d_head = pl.pallas_call(
+    )
+
+
+def finish():
+    return pl.pallas_call(
         finish_kernel,
         out_shape=(shape(48, 4 * KW), shape(48, HD), shape(48, HD), shape(48, HD), shape(32, C), shape(48, TRACKS)),
-        in_specs=[VMEM],
+        in_specs=[VMEM] * 2,
         out_specs=(VMEM,) * 6,
         compiler_params=params(),
         name="finish",
-    )(exchange(sent))
+    )
+
+
+def per_device(bases, targets, w_conv, w_query, w_key, w_value, w_out, w_head):
+    s = lax.axis_index("seq")
+    info = jnp.stack([lax.div(s, GROUP), lax.rem(s, GROUP)]).astype(jnp.int32)
+    groups = [list(range(GROUP)), list(range(GROUP, 2 * GROUP))]
+
+    def exchange(value):
+        return lax.all_to_all(value, "seq", 0, 0, axis_index_groups=groups, tiled=True)
+
+    targets_there = lax.ppermute(targets, "seq", [(i, i ^ GROUP) for i in range(2 * GROUP)])
+    every = lax.all_to_all(jnp.broadcast_to(bases.reshape(1, 2, 128), (16, 2, 128)), "seq", 0, 0, tiled=True)
+
+    x_own, hot_t, inverse, o_here, xh, xl, scales, qkv, w_t, slopes, eh, el = attend()(info, every, w_conv, w_query, w_key, w_value)
+    log_rate, do_sent, dy, grads = decode()(info, exchange(o_here), x_own, targets, targets_there, w_out, w_head)
+    grads = exchange(grads)
+    sent = attend_back()(info, exchange(do_sent), qkv, inverse, w_t, hot_t, scales, dy, eh, el, xh, xl, slopes)
+    sent, grads = lax.optimization_barrier((sent, grads))
+    d_conv, d_query, d_key, d_value, d_out, d_head = finish()(exchange(sent), grads)
     return (log_rate, jnp.transpose(d_conv), d_query, d_key, d_value, d_out, d_head)
 
 

time: 110 us -> 106 us (0.964)
  blocking collectives: 31.4 us -> 24.8 us
  starting transfers between devices: 12.5 us -> 16.2 us
    all_to_all x2, blocking collectives: 31.4 us -> 24.8 us  [exchange(): lax.all_to_all(value, 'seq', 0, 0, axis_index_groups=groups, tiled=True)]
    all_to_all x1 -> x2, starting transfers between devices: 3.42 us -> 7.16 us  [exchange(): lax.all_to_all(value, 'seq', 0, 0, axis_index_groups=groups, tiled=True)]
  transfers between devices with their start and end apart: 3 -> 4, of which waited for: 3 -> 3; matrix products, arithmetic and copies ran while one was open for 1% -> 1% of each run, Pallas kernels for 0% -> 17%
where the time goes in v3:
time: 106 us; the launch traced here: 105 us
  Pallas kernels  46.6 us (44%)
  blocking collectives  24.8 us (23%)
  starting transfers between devices  16.2 us (15%)
  waiting for transfers between devices  14 us (13%)
  local copies, waits for them, and re-layouts  2.61 us (2%)
    all_to_all x2, blocking collectives, exchange(): lax.all_to_all(value, 'seq', 0, 0, axis_index_groups=groups, tiled=True)  24.8 us
    pallas_call x1, Pallas kernels, per_device(): attend()(info, every, w_conv, w_query, w_key, w_value)  20.6 us
    pallas_call x1, Pallas kernels, per_device(): attend_back()  18.3 us
    all_to_all x1, starting transfers between devices, per_device(): lax.all_to_all(jnp.broadcast_to(bases.reshape(1, 2, 128), (16, 2, 128)),...  8.47 us
    all_to_all x1, waiting for transfers between devices, per_device(): lax.all_to_all(jnp.broadcast_to(bases.reshape(1, 2, 128), (16, 2, 128)),...  7.41 us
    all_to_all x2, starting transfers between devices, exchange(): lax.all_to_all(value, 'seq', 0, 0, axis_index_groups=groups, tiled=True)  7.16 us
    pallas_call x1, Pallas kernels, per_device(): decode()  5.44 us
    ppermute x1, waiting for transfers between devices, per_device(): lax.ppermute(targets, 'seq', [(i, i ^ GROUP) for i in range(2 * GROUP)])  4.47 us
  transfers between devices with their start and end apart: 4, of which 3 were waited for; matrix products, arithmetic and copies ran while one was open for 1% of the time, Pallas kernels for 17%

profile of v3, /device:TPU:16, one launch (start us, length us, event | category | flops | bytes accessed | tf_op | source)
XLA Modules:
  0.0 105.5 jit_solution(9582386636932870143)
XLA Ops:
  0.6 1.3 %broadcast_in_dim.8 = s32[16,2,128]{2,1,0:T(2,128)} broadcast(s32[2,128]{1,0:T(2,128)} %bitcast.12), dimensions={1,2} | broadcast | bytes 17408 | tf_op jit(solution)/shard_map/broadcast_in_dim | solution.py:492
  1.9 8.5 %all-to-all-start = ((s32[16,2,128]{2,1,0:T(2,128)}), s32[16,2,128]{2,1,0:T(2,128)S(1)}, u32[]{:S(2)}, u32[]{:S(2)}) async-start(s32[16,2,128]{2,1,0:T(2,128)} %broadcast_in_dim.8), calls=%async_computation | async-start | bytes 32768 | tf_op jit(solution)/shard_map/all_to_all | solution.py:492
  10.4 0.6 pad_add_fusion.info
  11.0 0.0 copy-start.3
  11.0 7.4 %all-to-all-done.bases = s32[16,2,128]{2,1,0:T(2,128)S(1)} async-done(((s32[16,2,128]{2,1,0:T(2,128)}), s32[16,2,128]{2,1,0:T(2,128)S(1)}, u32[]{:S(2)}, u32[]{:S(2)}) %all-to-all-start) | async-done | bytes 16416 | tf_op jit(solution)/shard_map/all_to_all | solution.py:492
  18.4 0.6 copy-done.2
  19.0 20.6 %attend.1 = (f32[128,768]{1,0:T(8,128)}, bf16[128,1024]{1,0:T(8,128)(2,1)}, f32[1,1024]{1,0:T(1,128)}, f32[512,128]{1,0:T(8,128)}, bf16[1024,768]{1,0:T(8,128)(2...) custom-call(s32[2]{0:T(128)} %pad_add_fusion.info, ...), custom_call_target="tpu_custom_call" | custom-call | tf_op jit(solution)/shard_map/attend/pallas_call | solution.py:494
  39.6 3.4 %all-to-all-start.1 = ((f32[8,64,128]{2,1,0:T(8,128)}), f32[8,64,128]{2,1,0:T(8,128)S(1)}, u32[]{:S(2)}, u32[]{:S(2)}) async-start(f32[8,64,128]{2,1,0:T(8,128)} %bitcast.10), calls=%async_computation.1 | async-start | bytes 524288 | tf_op jit(solution)/shard_map/all_to_all | solution.py:489
  43.0 0.0 copy-done.3
  43.0 0.5 collective-permute-start
  43.6 4.5 %collective-permute-done.targets_there = s32[64,128]{1,0:T(8,128)S(1)} collective-permute-done((s32[64,128]{1,0:T(8,128)S(1)}, s32[64,128]{1,0:T(8,128)S(1)}, u32[]{:S(2)}, u32[]{:S(2)}) %collective-permute-start) | collective-permute-done | bytes 32800 | tf_op jit(solution)/shard_map/ppermute | solution.py:491
  48.0 0.0 copy-start.4
  48.0 2.1 %all-to-all-done.1 = f32[8,64,128]{2,1,0:T(8,128)S(1)} async-done(((f32[8,64,128]{2,1,0:T(8,128)}), f32[8,64,128]{2,1,0:T(8,128)S(1)}, u32[]{:S(2)}, u32[]{:S(2)}) %all-to-all-start.1) | async-done | bytes 262176 | tf_op jit(solution)/shard_map/all_to_all | solution.py:489
  50.2 0.0 copy-done.4
  50.2 0.7 copy-done.1
  50.9 5.4 %decode.1 = (f32[64,128]{1,0:T(8,128)}, f32[512,128]{1,0:T(8,128)}, f32[128,768]{1,0:T(8,128)}, f32[8,240,128]{2,1,0:T(8,128)}) custom-call(s32[2]{0:T(128)} %pad_add_fusion.info, f32[512,128]{1,0:T(8,128)} %bitcast.9, f32[128,768]{1,0:T(8,128)} %get-tuple-element.32.x_own, s32[64,128]{1,0:T(8,128)} %targets_here.1, s32[64,128]{1,0:T(8,128)} %copy-done.4, ...), custom_call_target="tpu_custom_call" | custom-call | tf_op jit(solution)/shard_map/decode/pallas_call | solution.py:495
  56.3 11.3 %all_to_all.37 = f32[8,64,128]{2,1,0:T(8,128)} all-to-all(f32[8,64,128]{2,1,0:T(8,128)} %bitcast.11), channel_id=1, replica_groups={{0,16,32,48,64,80,96,112},{128,144,160,176,192,208,224,240},{1,17,33,49..., dimensions={0} | all-to-all | bytes 524288 | tf_op jit(solution)/shard_map/all_to_all | solution.py:489
  67.6 3.7 %all-to-all-start.3 = ((f32[8,240,128]{2,1,0:T(8,128)}), f32[8,240,128]{2,1,0:T(8,128)S(1)}, u32[]{:S(2)}, u32[]{:S(2)}) async-start(f32[8,240,128]{2,1,0:T(8,128)} %get-tuple-element.46), calls=%async_computation.3 | async-start | bytes 1966080 | tf_op jit(solution)/shard_map/all_to_all | solution.py:489
  71.4 18.3 %attend_back.1 = f32[8,96,128]{2,1,0:T(8,128)} custom-call(s32[2]{0:T(128)} %pad_add_fusion.info, f32[512,128]{1,0:T(8,128)} %bitcast.8, f32[1024,192]{1,0:T(8,128)} %get-tuple-element.35.qkv_ref, f32[1,1024]{1,0:T(1,128)} %get-tuple-element.36.inverse, f32[192,768]{1,0:T(8,128)} %get-tuple-element.37.w_t, bf16[128,1024]{1,0:T(8,128)(2,1)} %get-tuple-element.38.hot_t, ...), custom_call_target="tpu_custom_call" | custom-call | tf_op jit(solution)/shard_map/attend_back/pallas_call | solution.py:497
  89.7 0.0 all-to-all-done.3.grads
  89.7 0.0 copy-start
  89.7 13.6 %all_to_all.38.got = f32[8,96,128]{2,1,0:T(8,128)} all-to-all(f32[8,96,128]{2,1,0:T(8,128)} %attend_back.1), channel_id=1, replica_groups={{0,16,32,48,64,80,96,112},{128,144,160,176,192,208,224,240},{1,17,33,49..., dimensions={0} | all-to-all | bytes 786432 | tf_op jit(solution)/shard_map/all_to_all | solution.py:489
  103.3 0.0 copy-done
  103.3 2.2 %finish.1 = (f32[48,60]{1,0:T(8,128)}, f32[48,512]{1,0:T(8,128)}, f32[48,512]{1,0:T(8,128)}, f32[48,512]{1,0:T(8,128)}, f32[32,768]{1,0:T(8,128)}, /*index=5*/f32[48,128]{1,0:T(8,128)}) custom-call(f32[8,96,128]{2,1,0:T(8,128)} %all_to_all.38.got, f32[8,240,128]{2,1,0:T(8,128)} %copy-done), custom_call_target="tpu_custom_call" | custom-call | tf_op jit(solution)/shard_map/finish/pallas_call | solution.py:499
  (2 shorter events, 0.0 us)
Async XLA Ops:
  1.9 16.5 %all-to-all-start = ((s32[16,2,128]{2,1,0:T(2,128)}), s32[16,2,128]{2,1,0:T(2,128)S(1)}, u32[]{:S(2)}, u32[]{:S(2)}) async-start(s32[16,2,128]{2,1,0:T(2,128)} %broadcast_in_dim.8), calls=%async_computation | async-start | bytes 32768 | tf_op jit(solution)/shard_map/all_to_all | solution.py:492
  11.0 32.0 %copy-start.3 = (s32[64,128]{1,0:T(8,128)S(1)}, s32[64,128]{1,0:T(8,128)}, u32[]{:S(2)}) copy-start(s32[64,128]{1,0:T(8,128)} %targets_here.1) | copy-start | bytes 98308
  18.4 0.6 copy-start.2
  39.6 10.6 %all-to-all-start.1 = ((f32[8,64,128]{2,1,0:T(8,128)}), f32[8,64,128]{2,1,0:T(8,128)S(1)}, u32[]{:S(2)}, u32[]{:S(2)}) async-start(f32[8,64,128]{2,1,0:T(8,128)} %bitcast.10), calls=%async_computation.1 | async-start | bytes 524288 | tf_op jit(solution)/shard_map/all_to_all | solution.py:489
  43.0 5.0 %collective-permute-start = (s32[64,128]{1,0:T(8,128)S(1)}, s32[64,128]{1,0:T(8,128)S(1)}, u32[]{:S(2)}, u32[]{:S(2)}) collective-permute-start(s32[64,128]{1,0:T(8,128)S(1)} %copy-done.3), channel_id=1, source_target_pairs={{0,128},{16,144},{32,160},{48,176},{64,192},{80,208},{96,224},{112... | collective-permute-start | bytes 98312 | tf_op jit(solution)/shard_map/ppermute | solution.py:491
  48.0 2.1 %copy-start.4 = (s32[64,128]{1,0:T(8,128)}, s32[64,128]{1,0:T(8,128)S(1)}, u32[]{:S(2)}) copy-start(s32[64,128]{1,0:T(8,128)S(1)} %collective-permute-done.targets_there) | copy-start | bytes 98308
  50.2 0.7 copy-start.1
  67.6 22.1 %all-to-all-start.3 = ((f32[8,240,128]{2,1,0:T(8,128)}), f32[8,240,128]{2,1,0:T(8,128)S(1)}, u32[]{:S(2)}, u32[]{:S(2)}) async-start(f32[8,240,128]{2,1,0:T(8,128)} %get-tuple-element.46), calls=%async_computation.3 | async-start | bytes 1966080 | tf_op jit(solution)/shard_map/all_to_all | solution.py:489
  89.7 13.6 %copy-start = (f32[8,240,128]{2,1,0:T(8,128)}, f32[8,240,128]{2,1,0:T(8,128)S(1)}, u32[]{:S(2)}) copy-start(f32[8,240,128]{2,1,0:T(8,128)S(1)} %all-to-all-done.3.grads) | copy-start | bytes 2949124

commit v4 on v3

--- a/solution.py
+++ b/solution.py
@@ -107,7 +107,7 @@
 def attend_kernel(
     info, bases, w_conv, wq_hbm, wk_hbm, wv_hbm,
     x_own, hot_t, inverse, o_out, xh_hbm, xl_hbm, scale_hbm, qkv_hbm, w_t_hbm, slopes_hbm, eh_hbm, el_hbm,
-    pad, w_all, window, slabs, x_all, xh_out, xl_out, scale_out, qkv_out, w_t, slopes, eh_all, el_all, sems, slope_sems, e_sems, out_sems,
+    pad, w_all, window, slabs, x_all, xh_out, xl_out, scale_out, qkv_out, w_t, slopes, eh_all, el_all, sems, slope_sems, e_sems, out_sems, chunk_sems,
 ):
     half, m = info[0], info[1]
     copies = []
@@ -150,17 +150,16 @@
         total = None
         for r in range(POOL):
             y = dot(hot, w_all[:, r * C:(r + 1) * C])
-            b = y * y * GELU_C
-            t = jnp.tanh(y + y * b)
+            cube = y * (y * y * GELU_C)
+            t = jnp.tanh(y + cube)
             up = 1.0 + t
             total = y * up if total is None else total + y * up
-            slopes[here, r * C:(r + 1) * C] = up + (1.0 - t * t) * (y + y * (3.0 * b))
+            slopes[here, r * C:(r + 1) * C] = up + (1.0 - t * t) * (y + 3.0 * cube)
         x_all[here, :] = total * (0.5 / (GELU_A * POOL))
         hot_t[:, here] = jnp.transpose(hot[:, :128].astype(F32)).astype(BF16)
         pltpu.make_async_copy(slopes.at[here], slopes_hbm.at[here], slope_sems.at[c]).start()
         return 0
 
-    lax.fori_loop(0, steps, encode, 0)
     for copy in copies:
         copy.wait()
     odd = lax.rem(m, 2) == 1
@@ -168,6 +167,8 @@
     w_t[...] = jnp.transpose(jnp.concatenate(columns, axis=1))
     w_qkv = jnp.concatenate([columns[0] * HS ** -0.5, columns[1], columns[2]], axis=1)
     wh, wm, wl = split3(w_qkv)
+
+    chunked = ((xh_out, xh_hbm), (xl_out, xl_hbm), (scale_out, scale_hbm))
 
     def project(c, _):
         here = pl.ds(pl.multiple_of(c * TILE, TILE), TILE)
@@ -178,17 +179,27 @@
         h, mid, low = split3(xn)
         xh_out[here, :] = h
         xl_out[here, :] = mid
+        for i, (a, b) in enumerate(chunked):
+            pltpu.make_async_copy(a.at[here], b.at[here], chunk_sems.at[i, c]).start()
         qkv_out[here, :] = dot(h, wh) + ((dot(h, wm) + dot(mid, wh)) + (dot(mid, wm) + (dot(h, wl) + dot(low, wh))))
         return 0
 
-    lax.fori_loop(0, steps, project, 0)
+    encode(0, 0)
+
+    def both_steps(c, _):
+        project(c - 1, 0)
+        encode(c, 0)
+        return 0
+
+    lax.fori_loop(1, steps, both_steps, 0)
+    project(steps - 1, 0)
     for part in range(2):
         here = pl.ds(pl.multiple_of(part * 512 + m * OWN, OWN), OWN)
         x_own[part * OWN:(part + 1) * OWN, :] = x_all[here, :]
 
     outs_copies = [
         pltpu.make_async_copy(a, b, out_sems.at[i])
-        for i, (a, b) in enumerate(((xh_out, xh_hbm), (xl_out, xl_hbm), (scale_out, scale_hbm), (qkv_out, qkv_hbm), (w_t, w_t_hbm)))
+        for i, (a, b) in enumerate(((qkv_out, qkv_hbm), (w_t, w_t_hbm)))
     ]
     for copy in outs_copies:
         copy.start()
@@ -198,8 +209,11 @@
     vh, vl = split2(jnp.transpose(qkv[:, 2 * HS:]))
     v_both = jnp.concatenate([vh, vl], axis=0)
     outs = []
+    following = dot(keys, q_t[:, :TILE])
     for c in range(steps):
-        scores = dot(keys, q_t[:, c * TILE:(c + 1) * TILE])
+        scores = following
+        if c + 1 < steps:
+            following = dot(keys, q_t[:, (c + 1) * TILE:(c + 2) * TILE])
         e = jnp.exp(scores - jnp.max(scores, axis=0, keepdims=True))
         eh, el = split2(e)
         over = 1.0 / jnp.sum(eh.astype(F32) + el.astype(F32), axis=0, keepdims=True)
@@ -217,16 +231,17 @@
         copy.wait()
     for c in range(steps):
         here = pl.ds(c * TILE, TILE)
+        for i, (a, b) in enumerate(chunked):
+            pltpu.make_async_copy(a.at[here], b.at[here], chunk_sems.at[i, c]).wait()
         pltpu.make_async_copy(slopes.at[here], slopes_hbm.at[here], slope_sems.at[c]).wait()
         pltpu.make_async_copy(eh_all.at[c], eh_hbm.at[c], e_sems.at[0, c]).wait()
         pltpu.make_async_copy(el_all.at[c], el_hbm.at[c], e_sems.at[1, c]).wait()
 
 
 def decode_kernel(
-    info, o_parts, x_own, targets_here, targets_there, w_out, w_head,
-    log_rate, do_out, dy_out, grads_hbm, yn_all, grads_out, sem,
+    o_parts, x_own, targets_here, targets_there, w_out, w_head,
+    log_rate, do_out, dy_out, yn_all, d_rate_out,
 ):
-    half = info[0]
     parts = [o_parts[h * OWN:(h + 1) * OWN, :] for h in range(HEADS)]
     attended = jnp.concatenate(
         [jnp.concatenate([p[:, :HS] for p in parts], axis=1), jnp.concatenate([p[:, HS:] for p in parts], axis=1)], axis=0
@@ -243,9 +258,18 @@
     log_rate[...] = rate[:OWN]
     targets = jnp.concatenate([targets_here[...], targets_there[...]], axis=0).astype(F32)
     d_rate = (jnp.exp(rate) - targets) * (1.0 / math.sqrt(TOKENS))
+    d_rate_out[...] = d_rate
     d_yn = dot3_thin(d_rate, jnp.transpose(w_head[...]))
     dy = scale * (d_yn - yn * jnp.mean(d_yn * yn, axis=-1, keepdims=True))
     dy_out[...] = dy
+    dth, dtl = split2(jnp.transpose(dy))
+    both = dot(wouth, jnp.concatenate([dth, dtl], axis=1))
+    do_out[...] = both[:, :2 * OWN] + (both[:, 2 * OWN:] + dot(woutl, dth))
+
+
+def share_kernel(info, o_parts, dy, yn_all, d_rate_ref, grads_out):
+    half = info[0]
+    d_rate = d_rate_ref[...]
     heads = o_parts[pl.ds(pl.multiple_of(half * 256, 256), 256), :]
     o_t = jnp.concatenate(
         [
@@ -256,25 +280,19 @@
         ],
         axis=0,
     )
-    d_out = dot3_thin(o_t, dy)
+    d_out = dot3_thin(o_t, dy[...])
     yn_half = yn_all[:, pl.ds(pl.multiple_of(half * 384, 128), 384)]
     d_head = dot3_thin(jnp.transpose(yn_half), d_rate)
     for p in range(GROUP):
         for j in range(6):
             grads_out[p, 32 * j:32 * j + 32, :] = d_out[32 * p:32 * p + 32, 128 * j:128 * j + 128]
         grads_out[p, 192:240, :] = d_head[48 * p:48 * p + 48, :]
-    copy = pltpu.make_async_copy(grads_out, grads_hbm, sem)
-    copy.start()
-    dth, dtl = split2(jnp.transpose(dy))
-    both = dot(wouth, jnp.concatenate([dth, dtl], axis=1))
-    do_out[...] = both[:, :2 * OWN] + (both[:, 2 * OWN:] + dot(woutl, dth))
-    copy.wait()
 
 
 def attend_back_kernel(
-    info, do_parts, qkv_ref, inverse, w_t, hot_t, scales, dy, eh_hbm, el_hbm, xh_hbm, xl_hbm, slopes_hbm,
+    info, do_parts, qkv_ref, inverse, w_t_hbm, hot_t_hbm, scales_hbm, dy_hbm, eh_hbm, el_hbm, xh_hbm, xl_hbm, slopes_hbm,
     sent,
-    eh_all, el_all, xh, xl, slopes, do_all, g_t, dk_acc, dv_acc, dy_all, conv_acc, dconv, sems, e_sems,
+    w_t, hot_t, scales, dy, eh_all, el_all, xh, xl, slopes, do_all, g_t, dk_acc, dv_acc, dy_all, conv_acc, dconv, sems, e_sems,
 ):
     half, m = info[0], info[1]
     steps = TOKENS // TILE
@@ -282,9 +300,9 @@
         [pltpu.make_async_copy(there.at[c], here.at[c], e_sems.at[i, c]) for i, (there, here) in enumerate(((eh_hbm, eh_all), (el_hbm, el_all)))]
         for c in range(steps)
     ]
-    copies = [pltpu.make_async_copy(a, b, sems.at[i]) for i, (a, b) in enumerate(((xh_hbm, xh), (xl_hbm, xl)))]
+    copies = [pltpu.make_async_copy(a, b, sems.at[i]) for i, (a, b) in enumerate(((dy_hbm, dy), (xh_hbm, xh), (xl_hbm, xl), (w_t_hbm, w_t), (hot_t_hbm, hot_t), (scales_hbm, scales)))]
     copies += [
-        pltpu.make_async_copy(slopes_hbm.at[pl.ds(c * TILE, TILE)], slopes.at[pl.ds(c * TILE, TILE)], sems.at[2 + c]) for c in range(steps)
+        pltpu.make_async_copy(slopes_hbm.at[pl.ds(c * TILE, TILE)], slopes.at[pl.ds(c * TILE, TILE)], sems.at[6 + c]) for c in range(steps)
     ]
     for pair in e_copies:
         for copy in pair:
@@ -308,11 +326,12 @@
     qh, ql = split2(qkv[:, :HS])
     q_both = jnp.concatenate([qh, ql], axis=1)
     dy_all[...] = jnp.zeros_like(dy_all)
-    for part in range(2):
-        dy_all[pl.ds(pl.multiple_of(part * 512 + m * OWN, OWN), OWN), :] = dy[part * OWN:(part + 1) * OWN, :]
+    following = dot(v_three, do_t[:, :TILE])
     for c in range(steps):
         here = slice(c * TILE, (c + 1) * TILE)
-        dp = dot(v_three, do_t[:, here])
+        dp = following
+        if c + 1 < steps:
+            following = dot(v_three, do_t[:, (c + 1) * TILE:(c + 2) * TILE])
         for copy in e_copies[c]:
             copy.wait()
         eh, el = eh_all[c], el_all[c]
@@ -333,8 +352,10 @@
             dv_acc[...] += dv
     g_t[HS:2 * HS, :] = jnp.transpose(dk_acc[...])
     g_t[2 * HS:3 * HS, :] = jnp.transpose(dv_acc[...])
-    copies[0].wait()
-    copies[1].wait()
+    for copy in copies[:6]:
+        copy.wait()
+    for part in range(2):
+        dy_all[pl.ds(pl.multiple_of(part * 512 + m * OWN, OWN), OWN), :] = dy[part * OWN:(part + 1) * OWN, :]
     lanes = pl.ds(pl.multiple_of(half * 384, 128), 384)
     gh, gl = split2(g_t[...])
     both = dot(jnp.concatenate([gh, gl], axis=0), xh[:, lanes])
@@ -342,19 +363,25 @@
 
     wh, wl = split2(w_t[...])
     w_three = jnp.concatenate([wh, wl, wh], axis=0)
+
+    def back_to_xn(c):
+        gh, gl = split2(jnp.transpose(g_t[:, c * TILE:(c + 1) * TILE]))
+        return dot(jnp.concatenate([gh, gh, gl], axis=1), w_three)
+
+    following = back_to_xn(0)
     for c in range(steps):
         here = slice(c * TILE, (c + 1) * TILE)
-        gh, gl = split2(jnp.transpose(g_t[:, here]))
-        d_xn = dot(jnp.concatenate([gh, gh, gl], axis=1), w_three)
+        d_xn = following
+        if c + 1 < steps:
+            following = back_to_xn(c + 1)
         xn = xh[here].astype(F32) + xl[here].astype(F32)
         mean = jnp.mean(d_xn * xn, axis=-1, keepdims=True)
         d_x = (dy_all[here] + scales[here, :1] * (d_xn - xn * mean)) * (0.5 / POOL)
-        copies[2 + c].wait()
+        copies[6 + c].wait()
         hot = hot_t[:, here]
-        hot_two = jnp.concatenate([hot, hot], axis=1)
         for r in range(POOL):
             dh, dl = split2(d_x * slopes[here, r * C:(r + 1) * C])
-            moved = dot(hot_two, jnp.concatenate([dh, dl], axis=0))
+            moved = dot(hot, dh) + dot(hot, dl)
             if c == 0:
                 conv_acc[r] = moved
             else:
@@ -373,15 +400,19 @@
         sent[p, 72:96, :] = jnp.concatenate([mine[:24], mine[24:]], axis=1)
 
 
-def finish_kernel(got, grads, d_conv, d_query, d_key, d_value, d_out, d_head):
-    total = got[0, 72:96, :]
+def sum_kernel(grads, d_out, d_head):
     every = grads[0]
     for p in range(1, GROUP):
-        total = total + got[p, 72:96, :]
         every = every + grads[p]
-    d_conv[...] = jnp.concatenate([total[:, :HS], total[:, HS:]], axis=0)[:, :4 * KW]
     d_out[...] = jnp.concatenate([every[32 * j:32 * j + 32, :] for j in range(6)], axis=1)
     d_head[...] = every[192:240, :]
+
+
+def finish_kernel(got, d_conv, d_query, d_key, d_value):
+    total = got[0, 72:96, :]
+    for p in range(1, GROUP):
+        total = total + got[p, 72:96, :]
+    d_conv[...] = jnp.concatenate([total[:, :HS], total[:, HS:]], axis=0)[:, :4 * KW]
     for part, out in enumerate((d_query, d_key)):
         out[...] = jnp.concatenate([got[h, 0:48, part * HS:(part + 1) * HS] for h in range(HEADS)], axis=1)
     rows = [got[h, 48:72, :] for h in range(HEADS)]
@@ -423,7 +454,8 @@
             pltpu.SemaphoreType.DMA((3,)),
             pltpu.SemaphoreType.DMA((4,)),
             pltpu.SemaphoreType.DMA((2, 4)),
-            pltpu.SemaphoreType.DMA((5,)),
+            pltpu.SemaphoreType.DMA((2,)),
+            pltpu.SemaphoreType.DMA((3, 4)),
         ],
         compiler_params=params(),
         name="attend",
@@ -433,12 +465,22 @@
 def decode():
     return pl.pallas_call(
         decode_kernel,
-        out_shape=(shape(OWN, TRACKS), shape(HD, 128), shape(2 * OWN, C), shape(GROUP, 240, 128)),
-        in_specs=[SMEM] + [VMEM] * 6,
-        out_specs=(VMEM,) * 3 + (ANY,),
-        scratch_shapes=[pltpu.VMEM((2 * OWN, C), F32), pltpu.VMEM((GROUP, 240, 128), F32), pltpu.SemaphoreType.DMA],
-        compiler_params=params(),
+        out_shape=(shape(OWN, TRACKS), shape(HD, 128), shape(2 * OWN, C), shape(2 * OWN, C), shape(2 * OWN, TRACKS)),
+        in_specs=[VMEM] * 6,
+        out_specs=(VMEM,) * 5,
+        compiler_params=params(16),
         name="decode",
+    )
+
+
+def share():
+    return pl.pallas_call(
+        share_kernel,
+        out_shape=shape(GROUP, 240, 128),
+        in_specs=[SMEM] + [VMEM] * 4,
+        out_specs=VMEM,
+        compiler_params=params(16),
+        name="share",
     )
 
 
@@ -446,9 +488,13 @@
     return pl.pallas_call(
         attend_back_kernel,
         out_shape=shape(GROUP, 96, 128),
-        in_specs=[SMEM] + [VMEM] * 7 + [ANY] * 5,
+        in_specs=[SMEM] + [VMEM] * 3 + [ANY] * 9,
         out_specs=VMEM,
         scratch_shapes=[
+            pltpu.VMEM((3 * HS, C), F32),
+            pltpu.VMEM((128, TOKENS), BF16),
+            pltpu.VMEM((TOKENS, 128), F32),
+            pltpu.VMEM((2 * OWN, C), F32),
             pltpu.VMEM((4, TOKENS, TILE), BF16),
             pltpu.VMEM((4, TOKENS, TILE), BF16),
             pltpu.VMEM((TOKENS, C), BF16),
@@ -461,7 +507,7 @@
             pltpu.VMEM((TOKENS, C), F32),
             pltpu.VMEM((POOL, 128, C), F32),
             pltpu.VMEM((128, C), F32),
-            pltpu.SemaphoreType.DMA((6,)),
+            pltpu.SemaphoreType.DMA((10,)),
             pltpu.SemaphoreType.DMA((2, 4)),
         ],
         compiler_params=params(),
@@ -469,13 +515,24 @@
     )
 
 
+def add_up():
+    return pl.pallas_call(
+        sum_kernel,
+        out_shape=(shape(32, C), shape(48, TRACKS)),
+        in_specs=[VMEM],
+        out_specs=(VMEM,) * 2,
+        compiler_params=params(8),
+        name="add_up",
+    )
+
+
 def finish():
     return pl.pallas_call(
         finish_kernel,
-        out_shape=(shape(48, 4 * KW), shape(48, HD), shape(48, HD), shape(48, HD), shape(32, C), shape(48, TRACKS)),
-        in_specs=[VMEM] * 2,
-        out_specs=(VMEM,) * 6,
-        compiler_params=params(),
+        out_shape=(shape(48, 4 * KW), shape(48, HD), shape(48, HD), shape(48, HD)),
+        in_specs=[VMEM],
+        out_specs=(VMEM,) * 4,
+        compiler_params=params(8),
         name="finish",
     )
 
@@ -491,12 +548,16 @@
     targets_there = lax.ppermute(targets, "seq", [(i, i ^ GROUP) for i in range(2 * GROUP)])
     every = lax.all_to_all(jnp.broadcast_to(bases.reshape(1, 2, 128), (16, 2, 128)), "seq", 0, 0, tiled=True)
 
+    every, targets_there = lax.optimization_barrier((every, targets_there))
     x_own, hot_t, inverse, o_here, xh, xl, scales, qkv, w_t, slopes, eh, el = attend()(info, every, w_conv, w_query, w_key, w_value)
-    log_rate, do_sent, dy, grads = decode()(info, exchange(o_here), x_own, targets, targets_there, w_out, w_head)
-    grads = exchange(grads)
-    sent = attend_back()(info, exchange(do_sent), qkv, inverse, w_t, hot_t, scales, dy, eh, el, xh, xl, slopes)
+    o_parts = exchange(o_here)
+    log_rate, do_sent, dy, yn, d_rate = decode()(o_parts, x_own, targets, targets_there, w_out, w_head)
+    do_parts = exchange(do_sent)
+    grads = exchange(share()(info, o_parts, dy, yn, d_rate))
+    sent = attend_back()(info, do_parts, qkv, inverse, w_t, hot_t, scales, dy, eh, el, xh, xl, slopes)
     sent, grads = lax.optimization_barrier((sent, grads))
-    d_conv, d_query, d_key, d_value, d_out, d_head = finish()(exchange(sent), grads)
+    d_out, d_head = add_up()(grads)
+    d_conv, d_query, d_key, d_value = finish()(exchange(sent))
     return (log_rate, jnp.transpose(d_conv), d_query, d_key, d_value, d_out, d_head)
 
 

time: 106 us -> 96.6 us (0.911)
  blocking collectives: 24.8 us -> 10.6 us
  starting transfers between devices: 16.2 us -> 23.9 us
  Pallas kernels: 46.6 us -> 40.7 us
  waiting for transfers between devices: 14 us -> 16.6 us
    all_to_all x2 -> x1, blocking collectives: 24.8 us -> 10.6 us  [exchange(): lax.all_to_all(value, 'seq', 0, 0, axis_index_groups=groups, tiled=True)]
    all_to_all x2 -> x3, waiting for transfers between devices: 2.14 us -> 12 us  [exchange(): lax.all_to_all(value, 'seq', 0, 0, axis_index_groups=groups, tiled=True)]
    all_to_all x2 -> x3, starting transfers between devices: 7.16 us -> 12.6 us  [exchange(): lax.all_to_all(value, 'seq', 0, 0, axis_index_groups=groups, tiled=True)]
    ppermute x1, waiting for transfers between devices: 4.47 us -> 0.01 us  [per_device(): lax.ppermute(targets, 'seq', [(i, i ^ GROUP) for i in range(2 * GROUP)])]
    all_to_all x1, waiting for transfers between devices: 7.41 us -> 4.58 us  [per_device(): lax.all_to_all(jnp.broadcast_to(bases.reshape(1, 2, 128), (16, 2, 128)),...]
    pallas_call x1, Pallas kernels: 20.6 us -> 17.8 us  [per_device(): attend()(info, every, w_conv, w_query, w_key, w_value)]
    ppermute x1, starting transfers between devices: 0.53 us -> 2.83 us  [per_device(): lax.ppermute(targets, 'seq', [(i, i ^ GROUP) for i in range(2 * GROUP)])]
    pallas_call x1, Pallas kernels: 18.3 us -> 16.6 us  [per_device(): attend_back()]
  transfers between devices with their start and end apart: 4 -> 5, of which waited for: 3 -> 3; matrix products, arithmetic and copies ran while one was open for 1% -> 1% of each run, Pallas kernels for 17% -> 20%
where the time goes in v4:
time: 96.6 us; the launch traced here: 96 us
  Pallas kernels  40.7 us (42%)
  starting transfers between devices  23.9 us (25%)
  waiting for transfers between devices  16.6 us (17%)
  blocking collectives  10.6 us (11%)
  local copies, waits for them, and re-layouts  2.9 us (3%)
    pallas_call x1, Pallas kernels, per_device(): attend()(info, every, w_conv, w_query, w_key, w_value)  17.8 us
    pallas_call x1, Pallas kernels, per_device(): attend_back()  16.6 us
    all_to_all x3, starting transfers between devices, exchange(): lax.all_to_all(value, 'seq', 0, 0, axis_index_groups=groups, tiled=True)  12.6 us
    all_to_all x3, waiting for transfers between devices, exchange(): lax.all_to_all(value, 'seq', 0, 0, axis_index_groups=groups, tiled=True)  12 us
    all_to_all x1, blocking collectives, exchange(): lax.all_to_all(value, 'seq', 0, 0, axis_index_groups=groups, tiled=True)  10.6 us
    all_to_all x1, starting transfers between devices, per_device(): lax.all_to_all(jnp.broadcast_to(bases.reshape(1, 2, 128), (16, 2, 128)),...  8.47 us
    all_to_all x1, waiting for transfers between devices, per_device(): lax.all_to_all(jnp.broadcast_to(bases.reshape(1, 2, 128), (16, 2, 128)),...  4.58 us
    ppermute x1, starting transfers between devices, per_device(): lax.ppermute(targets, 'seq', [(i, i ^ GROUP) for i in range(2 * GROUP)])  2.83 us
  transfers between devices with their start and end apart: 5, of which 3 were waited for; matrix products, arithmetic and copies ran while one was open for 1% of the time, Pallas kernels for 20%

profile of v4, /device:TPU:16, one launch (start us, length us, event | category | flops | bytes accessed | tf_op | source)
XLA Modules:
  0.0 96.0 jit_solution(9309125359066042247)
XLA Ops:
  0.6 1.3 %broadcast_in_dim.8 = s32[16,2,128]{2,1,0:T(2,128)} broadcast(s32[2,128]{1,0:T(2,128)} %bitcast.12), dimensions={1,2} | broadcast | bytes 17408 | tf_op jit(solution)/shard_map/broadcast_in_dim | solution.py:549
  1.9 8.5 %all-to-all-start = ((s32[16,2,128]{2,1,0:T(2,128)}), s32[16,2,128]{2,1,0:T(2,128)S(1)}, u32[]{:S(2)}, u32[]{:S(2)}) async-start(s32[16,2,128]{2,1,0:T(2,128)} %broadcast_in_dim.8), calls=%async_computation | async-start | bytes 32768 | tf_op jit(solution)/shard_map/all_to_all | solution.py:549
  10.4 2.8 %collective-permute-start = (s32[64,128]{1,0:T(8,128)}, s32[64,128]{1,0:T(8,128)S(1)}, u32[]{:S(2)}, u32[]{:S(2)}) collective-permute-start(s32[64,128]{1,0:T(8,128)} %targets_here.1), channel_id=1, source_target_pairs={{0,128},{16,144},{32,160},{48,176},{64,192},{80,208},{96,224},{112... | collective-permute-start | bytes 98312 | tf_op jit(solution)/shard_map/ppermute | solution.py:548
  13.2 0.6 pad_add_fusion.info
  13.8 4.6 %all-to-all-done.bases = s32[16,2,128]{2,1,0:T(2,128)S(1)} async-done(((s32[16,2,128]{2,1,0:T(2,128)}), s32[16,2,128]{2,1,0:T(2,128)S(1)}, u32[]{:S(2)}, u32[]{:S(2)}) %all-to-all-start) | async-done | bytes 16416 | tf_op jit(solution)/shard_map/all_to_all | solution.py:549
  18.4 0.0 collective-permute-done.targets_there
  18.4 0.6 copy-done.7
  19.0 17.8 %attend.1 = (f32[128,768]{1,0:T(8,128)}, bf16[128,1024]{1,0:T(8,128)(2,1)}, f32[1,1024]{1,0:T(1,128)}, f32[512,128]{1,0:T(8,128)}, bf16[1024,768]{1,0:T(8,128)(2...) custom-call(s32[2]{0:T(128)} %pad_add_fusion.info, ...), custom_call_target="tpu_custom_call" | custom-call | tf_op jit(solution)/shard_map/attend/pallas_call | solution.py:552
  36.8 10.6 %all_to_all.37 = f32[8,64,128]{2,1,0:T(8,128)S(1)} all-to-all(f32[8,64,128]{2,1,0:T(8,128)} %bitcast.11), channel_id=1, replica_groups={{0,16,32,48,64,80,96,112},{128,144,160,176,192,208,224,240},{1,17,33,49..., dimensions={0} | all-to-all | bytes 524288 | tf_op jit(solution)/shard_map/all_to_all | solution.py:546
  47.4 0.0 copy-done.4
  47.4 1.0 %copy-done.3 = f32[128,768]{1,0:T(8,128)S(1)} copy-done((f32[128,768]{1,0:T(8,128)S(1)}, f32[128,768]{1,0:T(8,128)}, u32[]{:S(2)}) %copy-start.3) | copy-done | bytes 393240
  48.4 2.7 %decode.1 = (f32[64,128]{1,0:T(8,128)}, f32[512,128]{1,0:T(8,128)}, f32[128,768]{1,0:T(8,128)S(1)}, f32[128,768]{1,0:T(8,128)S(1)}, f32[128,128]{1,0:T(8,128)S(1)}) custom-call(f32[512,128]{1,0:T(8,128)S(1)} %bitcast.8, f32[128,768]{1,0:T(8,128)S(1)} %copy-done.3, s32[64,128]{1,0:T(8,128)S(1)} %copy-done.4, ...), custom_call_target="tpu_custom_call" | custom-call | tf_op jit(solution)/shard_map/decode/pallas_call | solution.py:554
  51.0 3.4 %all-to-all-start.2 = ((f32[8,64,128]{2,1,0:T(8,128)}), f32[8,64,128]{2,1,0:T(8,128)S(1)}, u32[]{:S(2)}, u32[]{:S(2)}) async-start(f32[8,64,128]{2,1,0:T(8,128)} %bitcast.5), calls=%async_computation.2 | async-start | bytes 524288 | tf_op jit(solution)/shard_map/all_to_all | solution.py:546
  54.4 0.0 copy-done.5
  54.5 2.2 %share.1 = f32[8,240,128]{2,1,0:T(8,128)} custom-call(s32[2]{0:T(128)S(1)} %copy-done.5, f32[512,128]{1,0:T(8,128)S(1)} %bitcast.9, f32[128,768]{1,0:T(8,128)S(1)} %get-tuple-element.45.dy_hbm.dy, f32[128,768]{1,0:T(8,128)S(1)} %get-tuple-element.51.yn_all, f32[128,128]{1,0:T(8,128)S(1)} %get-tuple-element.52.d_rate_ref), custom_call_target="tpu_custom_call" | custom-call | tf_op jit(solution)/shard_map/share/pallas_call | solution.py:556
  56.7 4.9 %all-to-all-done.2 = f32[8,64,128]{2,1,0:T(8,128)S(1)} async-done(((f32[8,64,128]{2,1,0:T(8,128)}), f32[8,64,128]{2,1,0:T(8,128)S(1)}, u32[]{:S(2)}, u32[]{:S(2)}) %all-to-all-start.2) | async-done | bytes 262176 | tf_op jit(solution)/shard_map/all_to_all | solution.py:546
  61.6 0.0 copy-done.1
  61.6 3.7 %all-to-all-start.3 = ((f32[8,240,128]{2,1,0:T(8,128)}), f32[8,240,128]{2,1,0:T(8,128)S(1)}, u32[]{:S(2)}, u32[]{:S(2)}) async-start(f32[8,240,128]{2,1,0:T(8,128)} %share.1), calls=%async_computation.3 | async-start | bytes 1966080 | tf_op jit(solution)/shard_map/all_to_all | solution.py:546
  65.4 16.6 %attend_back.1 = f32[8,96,128]{2,1,0:T(8,128)} custom-call(s32[2]{0:T(128)} %pad_add_fusion.info, f32[512,128]{1,0:T(8,128)} %bitcast.10, f32[1024,192]{1,0:T(8,128)} %get-tuple-element.40.qkv_ref, f32[1,1024]{1,0:T(1,128)} %get-tuple-element.41.inverse, f32[192,768]{1,0:T(8,128)} %get-tuple-element.42.w_t_hbm, ...), custom_call_target="tpu_custom_call" | custom-call | tf_op jit(solution)/shard_map/attend_back/pallas_call | solution.py:557
  81.9 0.0 all-to-all-done.3.grads
  81.9 5.4 %all-to-all-start.4 = ((f32[8,96,128]{2,1,0:T(8,128)}), f32[8,96,128]{2,1,0:T(8,128)S(1)}, u32[]{:S(2)}, u32[]{:S(2)}) async-start(f32[8,96,128]{2,1,0:T(8,128)} %attend_back.1), calls=%async_computation.4 | async-start | bytes 786432 | tf_op jit(solution)/shard_map/all_to_all | solution.py:546
  87.4 0.7 add_up.1
  88.1 7.1 %all-to-all-done.4.got = f32[8,96,128]{2,1,0:T(8,128)S(1)} async-done(((f32[8,96,128]{2,1,0:T(8,128)}), f32[8,96,128]{2,1,0:T(8,128)S(1)}, u32[]{:S(2)}, u32[]{:S(2)}) %all-to-all-start.4) | async-done | bytes 393248 | tf_op jit(solution)/shard_map/all_to_all | solution.py:546
  95.1 0.8 finish.1
  (11 shorter events, 0.0 us)
Async XLA Ops:
  1.9 16.5 %all-to-all-start = ((s32[16,2,128]{2,1,0:T(2,128)}), s32[16,2,128]{2,1,0:T(2,128)S(1)}, u32[]{:S(2)}, u32[]{:S(2)}) async-start(s32[16,2,128]{2,1,0:T(2,128)} %broadcast_in_dim.8), calls=%async_computation | async-start | bytes 32768 | tf_op jit(solution)/shard_map/all_to_all | solution.py:549
  10.4 8.0 %collective-permute-start = (s32[64,128]{1,0:T(8,128)}, s32[64,128]{1,0:T(8,128)S(1)}, u32[]{:S(2)}, u32[]{:S(2)}) collective-permute-start(s32[64,128]{1,0:T(8,128)} %targets_here.1), channel_id=1, source_target_pairs={{0,128},{16,144},{32,160},{48,176},{64,192},{80,208},{96,224},{112... | collective-permute-start | bytes 98312 | tf_op jit(solution)/shard_map/ppermute | solution.py:548
  13.8 33.5 %copy-start = (f32[512,768]{1,0:T(8,128)S(1)}, f32[512,768]{1,0:T(8,128)}, u32[]{:S(2)}) copy-start(f32[512,768]{1,0:T(8,128)} %w_out.1) | copy-start | bytes 4718596
  13.8 33.5 %copy-start.2 = (f32[768,128]{1,0:T(8,128)S(1)}, f32[768,128]{1,0:T(8,128)}, u32[]{:S(2)}) copy-start(f32[768,128]{1,0:T(8,128)} %w_head.1) | copy-start | bytes 1179652
  13.8 33.5 %copy-start.4 = (s32[64,128]{1,0:T(8,128)S(1)}, s32[64,128]{1,0:T(8,128)}, u32[]{:S(2)}) copy-start(s32[64,128]{1,0:T(8,128)} %targets_here.1) | copy-start | bytes 98308
  18.4 0.6 copy-start.7
  47.4 1.0 %copy-start.3 = (f32[128,768]{1,0:T(8,128)S(1)}, f32[128,768]{1,0:T(8,128)}, u32[]{:S(2)}) copy-start(f32[128,768]{1,0:T(8,128)} %get-tuple-element.36.x_own) | copy-start | bytes 1179652
  48.4 6.1 %copy-start.5 = (s32[2]{0:T(128)S(1)}, s32[2]{0:T(128)}, u32[]{:S(2)}) copy-start(s32[2]{0:T(128)} %pad_add_fusion.info) | copy-start | bytes 28
  51.0 10.6 %copy-start.1 = (f32[128,768]{1,0:T(8,128)}, f32[128,768]{1,0:T(8,128)S(1)}, u32[]{:S(2)}) copy-start(f32[128,768]{1,0:T(8,128)S(1)} %get-tuple-element.45.dy_hbm.dy) | copy-start | bytes 1179652
  51.0 10.6 %all-to-all-start.2 = ((f32[8,64,128]{2,1,0:T(8,128)}), f32[8,64,128]{2,1,0:T(8,128)S(1)}, u32[]{:S(2)}, u32[]{:S(2)}) async-start(f32[8,64,128]{2,1,0:T(8,128)} %bitcast.5), calls=%async_computation.2 | async-start | bytes 524288 | tf_op jit(solution)/shard_map/all_to_all | solution.py:546
  61.6 3.8 %copy-start.6 = (f32[8,64,128]{2,1,0:T(8,128)}, f32[8,64,128]{2,1,0:T(8,128)S(1)}, u32[]{:S(2)}) copy-start(f32[8,64,128]{2,1,0:T(8,128)S(1)} %all-to-all-done.2) | copy-start | bytes 786436
  61.6 20.3 %all-to-all-start.3 = ((f32[8,240,128]{2,1,0:T(8,128)}), f32[8,240,128]{2,1,0:T(8,128)S(1)}, u32[]{:S(2)}, u32[]{:S(2)}) async-start(f32[8,240,128]{2,1,0:T(8,128)} %share.1), calls=%async_computation.3 | async-start | bytes 1966080 | tf_op jit(solution)/shard_map/all_to_all | solution.py:546
  81.9 13.2 %all-to-all-start.4 = ((f32[8,96,128]{2,1,0:T(8,128)}), f32[8,96,128]{2,1,0:T(8,128)S(1)}, u32[]{:S(2)}, u32[]{:S(2)}) async-start(f32[8,96,128]{2,1,0:T(8,128)} %attend_back.1), calls=%async_computation.4 | async-start | bytes 786432 | tf_op jit(solution)/shard_map/all_to_all | solution.py:546

commit v5 on v4

--- a/solution.py
+++ b/solution.py
@@ -290,9 +290,9 @@
 
 
 def attend_back_kernel(
-    info, do_parts, qkv_ref, inverse, w_t_hbm, hot_t_hbm, scales_hbm, dy_hbm, eh_hbm, el_hbm, xh_hbm, xl_hbm, slopes_hbm,
+    info, do_parts, qkv_hbm, inverse, w_t_hbm, hot_t_hbm, scales_hbm, dy_hbm, eh_hbm, el_hbm, xh_hbm, xl_hbm, slopes_hbm,
     sent,
-    w_t, hot_t, scales, dy, eh_all, el_all, xh, xl, slopes, do_all, g_t, dk_acc, dv_acc, dy_all, conv_acc, dconv, sems, e_sems,
+    qkv_ref, w_t, hot_t, scales, dy, eh_all, el_all, xh, xl, slopes, do_all, g_t, dk_acc, dv_acc, d_x_all, conv_acc, dconv, sems, e_sems,
 ):
     half, m = info[0], info[1]
     steps = TOKENS // TILE
@@ -304,6 +304,8 @@
     copies += [
         pltpu.make_async_copy(slopes_hbm.at[pl.ds(c * TILE, TILE)], slopes.at[pl.ds(c * TILE, TILE)], sems.at[6 + c]) for c in range(steps)
     ]
+    qkv_copy = pltpu.make_async_copy(qkv_hbm, qkv_ref, sems.at[10])
+    qkv_copy.start()
     for pair in e_copies:
         for copy in pair:
             copy.start()
@@ -313,6 +315,7 @@
         both = jnp.transpose(do_parts[p * OWN:(p + 1) * OWN, :])
         do_all[p * OWN:(p + 1) * OWN, :] = both[:OWN]
         do_all[512 + p * OWN:512 + (p + 1) * OWN, :] = both[OWN:]
+    qkv_copy.wait()
     qkv = qkv_ref[...]
     kh, kl = split2(jnp.transpose(qkv[:, HS:2 * HS]))
     k_both = jnp.concatenate([kh, kl], axis=0)
@@ -325,7 +328,6 @@
     do_both = jnp.concatenate([dh, dl], axis=1)
     qh, ql = split2(qkv[:, :HS])
     q_both = jnp.concatenate([qh, ql], axis=1)
-    dy_all[...] = jnp.zeros_like(dy_all)
     following = dot(v_three, do_t[:, :TILE])
     for c in range(steps):
         here = slice(c * TILE, (c + 1) * TILE)
@@ -354,8 +356,6 @@
     g_t[2 * HS:3 * HS, :] = jnp.transpose(dv_acc[...])
     for copy in copies[:6]:
         copy.wait()
-    for part in range(2):
-        dy_all[pl.ds(pl.multiple_of(part * 512 + m * OWN, OWN), OWN), :] = dy[part * OWN:(part + 1) * OWN, :]
     lanes = pl.ds(pl.multiple_of(half * 384, 128), 384)
     gh, gl = split2(g_t[...])
     both = dot(jnp.concatenate([gh, gl], axis=0), xh[:, lanes])
@@ -365,19 +365,23 @@
     w_three = jnp.concatenate([wh, wl, wh], axis=0)
 
     def back_to_xn(c):
-        gh, gl = split2(jnp.transpose(g_t[:, c * TILE:(c + 1) * TILE]))
+        gh, gl = split2(jnp.transpose(g_t[:, c * 512:(c + 1) * 512]))
         return dot(jnp.concatenate([gh, gh, gl], axis=1), w_three)
 
+    own = pl.ds(pl.multiple_of(m * OWN, OWN), OWN)
     following = back_to_xn(0)
-    for c in range(steps):
-        here = slice(c * TILE, (c + 1) * TILE)
+    for c in range(2):
+        here = slice(c * 512, (c + 1) * 512)
         d_xn = following
-        if c + 1 < steps:
+        if c + 1 < 2:
             following = back_to_xn(c + 1)
         xn = xh[here].astype(F32) + xl[here].astype(F32)
         mean = jnp.mean(d_xn * xn, axis=-1, keepdims=True)
-        d_x = (dy_all[here] + scales[here, :1] * (d_xn - xn * mean)) * (0.5 / POOL)
-        copies[6 + c].wait()
+        d_x_all[...] = scales[here, :1] * (d_xn - xn * mean) * (0.5 / POOL)
+        d_x_all[own, :] += dy[c * OWN:(c + 1) * OWN, :] * (0.5 / POOL)
+        d_x = d_x_all[...]
+        copies[6 + 2 * c].wait()
+        copies[7 + 2 * c].wait()
         hot = hot_t[:, here]
         for r in range(POOL):
             dh, dl = split2(d_x * slopes[here, r * C:(r + 1) * C])
@@ -488,9 +492,10 @@
     return pl.pallas_call(
         attend_back_kernel,
         out_shape=shape(GROUP, 96, 128),
-        in_specs=[SMEM] + [VMEM] * 3 + [ANY] * 9,
+        in_specs=[SMEM, VMEM, ANY, VMEM] + [ANY] * 9,
         out_specs=VMEM,
         scratch_shapes=[
+            pltpu.VMEM((TOKENS, 3 * HS), F32),
             pltpu.VMEM((3 * HS, C), F32),
             pltpu.VMEM((128, TOKENS), BF16),
             pltpu.VMEM((TOKENS, 128), F32),
@@ -504,10 +509,10 @@
             pltpu.VMEM((3 * HS, TOKENS), F32),
             pltpu.VMEM((TOKENS, HS), F32),
             pltpu.VMEM((TOKENS, HS), F32),
-            pltpu.VMEM((TOKENS, C), F32),
+            pltpu.VMEM((512, C), F32),
             pltpu.VMEM((POOL, 128, C), F32),
             pltpu.VMEM((128, C), F32),
-            pltpu.SemaphoreType.DMA((10,)),
+            pltpu.SemaphoreType.DMA((11,)),
             pltpu.SemaphoreType.DMA((2, 4)),
         ],
         compiler_params=params(),

time: 96.6 us -> 95.9 us (level)
  no operation moved by 1% of the time
where the time goes in v5:
time: 95.9 us; the launch traced here: 95.2 us
  Pallas kernels  40 us (42%)
  starting transfers between devices  23.9 us (25%)
  waiting for transfers between devices  16.6 us (17%)
  blocking collectives  10.6 us (11%)
  local copies, waits for them, and re-layouts  2.9 us (3%)
    pallas_call x1, Pallas kernels, per_device(): attend()(info, every, w_conv, w_query, w_key, w_value)  17.8 us
    pallas_call x1, Pallas kernels, per_device(): attend_back()  15.8 us
    all_to_all x3, starting transfers between devices, exchange(): lax.all_to_all(value, 'seq', 0, 0, axis_index_groups=groups, tiled=True)  12.6 us
    all_to_all x3, waiting for transfers between devices, exchange(): lax.all_to_all(value, 'seq', 0, 0, axis_index_groups=groups, tiled=True)  12 us
    all_to_all x1, blocking collectives, exchange(): lax.all_to_all(value, 'seq', 0, 0, axis_index_groups=groups, tiled=True)  10.6 us
    all_to_all x1, starting transfers between devices, per_device(): lax.all_to_all(jnp.broadcast_to(bases.reshape(1, 2, 128), (16, 2, 128)),...  8.47 us
    all_to_all x1, waiting for transfers between devices, per_device(): lax.all_to_all(jnp.broadcast_to(bases.reshape(1, 2, 128), (16, 2, 128)),...  4.58 us
    ppermute x1, starting transfers between devices, per_device(): lax.ppermute(targets, 'seq', [(i, i ^ GROUP) for i in range(2 * GROUP)])  2.83 us
  transfers between devices with their start and end apart: 5, of which 3 were waited for; matrix products, arithmetic and copies ran while one was open for 1% of the time, Pallas kernels for 20%

profile of v5, /device:TPU:16, one launch (start us, length us, event | category | flops | bytes accessed | tf_op | source)
XLA Modules:
  0.0 95.2 jit_solution(2129334692218844849)
XLA Ops:
  0.6 1.3 %broadcast_in_dim.8 = s32[16,2,128]{2,1,0:T(2,128)} broadcast(s32[2,128]{1,0:T(2,128)} %bitcast.12), dimensions={1,2} | broadcast | bytes 17408 | tf_op jit(solution)/shard_map/broadcast_in_dim | solution.py:554
  1.9 8.5 %all-to-all-start = ((s32[16,2,128]{2,1,0:T(2,128)}), s32[16,2,128]{2,1,0:T(2,128)S(1)}, u32[]{:S(2)}, u32[]{:S(2)}) async-start(s32[16,2,128]{2,1,0:T(2,128)} %broadcast_in_dim.8), calls=%async_computation | async-start | bytes 32768 | tf_op jit(solution)/shard_map/all_to_all | solution.py:554
  10.4 2.8 %collective-permute-start = (s32[64,128]{1,0:T(8,128)}, s32[64,128]{1,0:T(8,128)S(1)}, u32[]{:S(2)}, u32[]{:S(2)}) collective-permute-start(s32[64,128]{1,0:T(8,128)} %targets_here.1), channel_id=1, source_target_pairs={{0,128},{16,144},{32,160},{48,176},{64,192},{80,208},{96,224},{112... | collective-permute-start | bytes 98312 | tf_op jit(solution)/shard_map/ppermute | solution.py:553
  13.2 0.6 pad_add_fusion.info
  13.8 4.6 %all-to-all-done.bases = s32[16,2,128]{2,1,0:T(2,128)S(1)} async-done(((s32[16,2,128]{2,1,0:T(2,128)}), s32[16,2,128]{2,1,0:T(2,128)S(1)}, u32[]{:S(2)}, u32[]{:S(2)}) %all-to-all-start) | async-done | bytes 16416 | tf_op jit(solution)/shard_map/all_to_all | solution.py:554
  18.4 0.0 collective-permute-done.targets_there
  18.4 0.6 copy-done.7
  19.0 17.8 %attend.1 = (f32[128,768]{1,0:T(8,128)}, bf16[128,1024]{1,0:T(8,128)(2,1)}, f32[1,1024]{1,0:T(1,128)}, f32[512,128]{1,0:T(8,128)}, bf16[1024,768]{1,0:T(8,128)(2...) custom-call(s32[2]{0:T(128)} %pad_add_fusion.info, ...), custom_call_target="tpu_custom_call" | custom-call | tf_op jit(solution)/shard_map/attend/pallas_call | solution.py:557
  36.8 10.6 %all_to_all.37 = f32[8,64,128]{2,1,0:T(8,128)S(1)} all-to-all(f32[8,64,128]{2,1,0:T(8,128)} %bitcast.11), channel_id=1, replica_groups={{0,16,32,48,64,80,96,112},{128,144,160,176,192,208,224,240},{1,17,33,49..., dimensions={0} | all-to-all | bytes 524288 | tf_op jit(solution)/shard_map/all_to_all | solution.py:551
  47.4 0.0 copy-done
  47.4 0.0 copy-done.2
  47.4 0.0 copy-done.4
  47.4 1.0 %copy-done.3 = f32[128,768]{1,0:T(8,128)S(1)} copy-done((f32[128,768]{1,0:T(8,128)S(1)}, f32[128,768]{1,0:T(8,128)}, u32[]{:S(2)}) %copy-start.3) | copy-done | bytes 393240
  48.4 2.7 %decode.1 = (f32[64,128]{1,0:T(8,128)}, f32[512,128]{1,0:T(8,128)}, f32[128,768]{1,0:T(8,128)S(1)}, f32[128,768]{1,0:T(8,128)S(1)}, f32[128,128]{1,0:T(8,128)S(1)}) custom-call(f32[512,128]{1,0:T(8,128)S(1)} %bitcast.8, f32[128,768]{1,0:T(8,128)S(1)} %copy-done.3, s32[64,128]{1,0:T(8,128)S(1)} %copy-done.4, ...), custom_call_target="tpu_custom_call" | custom-call | tf_op jit(solution)/shard_map/decode/pallas_call | solution.py:559
  51.0 3.4 %all-to-all-start.2 = ((f32[8,64,128]{2,1,0:T(8,128)}), f32[8,64,128]{2,1,0:T(8,128)S(1)}, u32[]{:S(2)}, u32[]{:S(2)}) async-start(f32[8,64,128]{2,1,0:T(8,128)} %bitcast.5), calls=%async_computation.2 | async-start | bytes 524288 | tf_op jit(solution)/shard_map/all_to_all | solution.py:551
  54.5 2.2 %share.1 = f32[8,240,128]{2,1,0:T(8,128)} custom-call(s32[2]{0:T(128)S(1)} %copy-done.5, f32[512,128]{1,0:T(8,128)S(1)} %bitcast.9, f32[128,768]{1,0:T(8,128)S(1)} %get-tuple-element.45.dy_hbm.dy, f32[128,768]{1,0:T(8,128)S(1)} %get-tuple-element.51.yn_all, f32[128,128]{1,0:T(8,128)S(1)} %get-tuple-element.52.d_rate_ref), custom_call_target="tpu_custom_call" | custom-call | tf_op jit(solution)/shard_map/share/pallas_call | solution.py:561
  56.7 4.9 %all-to-all-done.2 = f32[8,64,128]{2,1,0:T(8,128)S(1)} async-done(((f32[8,64,128]{2,1,0:T(8,128)}), f32[8,64,128]{2,1,0:T(8,128)S(1)}, u32[]{:S(2)}, u32[]{:S(2)}) %all-to-all-start.2) | async-done | bytes 262176 | tf_op jit(solution)/shard_map/all_to_all | solution.py:551
  61.6 3.7 %all-to-all-start.3 = ((f32[8,240,128]{2,1,0:T(8,128)}), f32[8,240,128]{2,1,0:T(8,128)S(1)}, u32[]{:S(2)}, u32[]{:S(2)}) async-start(f32[8,240,128]{2,1,0:T(8,128)} %share.1), calls=%async_computation.3 | async-start | bytes 1966080 | tf_op jit(solution)/shard_map/all_to_all | solution.py:551
  65.4 15.8 %attend_back.1 = f32[8,96,128]{2,1,0:T(8,128)} custom-call(s32[2]{0:T(128)} %pad_add_fusion.info, f32[512,128]{1,0:T(8,128)} %bitcast.10, f32[1024,192]{1,0:T(8,128)} %get-tuple-element.40.qkv_hbm, f32[1,1024]{1,0:T(1,128)} %get-tuple-element.41.inverse, f32[192,768]{1,0:T(8,128)} %get-tuple-element.42.w_t_hbm, ...), custom_call_target="tpu_custom_call" | custom-call | tf_op jit(solution)/shard_map/attend_back/pallas_call | solution.py:562
  81.2 0.0 all-to-all-done.3.grads
  81.2 5.5 %all-to-all-start.4 = ((f32[8,96,128]{2,1,0:T(8,128)}), f32[8,96,128]{2,1,0:T(8,128)S(1)}, u32[]{:S(2)}, u32[]{:S(2)}) async-start(f32[8,96,128]{2,1,0:T(8,128)} %attend_back.1), calls=%async_computation.4 | async-start | bytes 786432 | tf_op jit(solution)/shard_map/all_to_all | solution.py:551
  86.7 0.7 add_up.1
  87.4 7.1 %all-to-all-done.4.got = f32[8,96,128]{2,1,0:T(8,128)S(1)} async-done(((f32[8,96,128]{2,1,0:T(8,128)}), f32[8,96,128]{2,1,0:T(8,128)S(1)}, u32[]{:S(2)}, u32[]{:S(2)}) %all-to-all-start.4) | async-done | bytes 393248 | tf_op jit(solution)/shard_map/all_to_all | solution.py:551
  94.4 0.8 finish.1
  (11 shorter events, 0.0 us)
Async XLA Ops:
  1.9 16.5 %all-to-all-start = ((s32[16,2,128]{2,1,0:T(2,128)}), s32[16,2,128]{2,1,0:T(2,128)S(1)}, u32[]{:S(2)}, u32[]{:S(2)}) async-start(s32[16,2,128]{2,1,0:T(2,128)} %broadcast_in_dim.8), calls=%async_computation | async-start | bytes 32768 | tf_op jit(solution)/shard_map/all_to_all | solution.py:554
  10.4 8.0 %collective-permute-start = (s32[64,128]{1,0:T(8,128)}, s32[64,128]{1,0:T(8,128)S(1)}, u32[]{:S(2)}, u32[]{:S(2)}) collective-permute-start(s32[64,128]{1,0:T(8,128)} %targets_here.1), channel_id=1, source_target_pairs={{0,128},{16,144},{32,160},{48,176},{64,192},{80,208},{96,224},{112... | collective-permute-start | bytes 98312 | tf_op jit(solution)/shard_map/ppermute | solution.py:553
  13.8 33.5 %copy-start = (f32[512,768]{1,0:T(8,128)S(1)}, f32[512,768]{1,0:T(8,128)}, u32[]{:S(2)}) copy-start(f32[512,768]{1,0:T(8,128)} %w_out.1) | copy-start | bytes 4718596
  13.8 33.5 %copy-start.2 = (f32[768,128]{1,0:T(8,128)S(1)}, f32[768,128]{1,0:T(8,128)}, u32[]{:S(2)}) copy-start(f32[768,128]{1,0:T(8,128)} %w_head.1) | copy-start | bytes 1179652
  13.8 33.5 %copy-start.4 = (s32[64,128]{1,0:T(8,128)S(1)}, s32[64,128]{1,0:T(8,128)}, u32[]{:S(2)}) copy-start(s32[64,128]{1,0:T(8,128)} %targets_here.1) | copy-start | bytes 98308
  18.4 0.6 copy-start.7
  47.4 1.0 %copy-start.3 = (f32[128,768]{1,0:T(8,128)S(1)}, f32[128,768]{1,0:T(8,128)}, u32[]{:S(2)}) copy-start(f32[128,768]{1,0:T(8,128)} %get-tuple-element.36.x_own) | copy-start | bytes 1179652
  48.4 6.1 %copy-start.5 = (s32[2]{0:T(128)S(1)}, s32[2]{0:T(128)}, u32[]{:S(2)}) copy-start(s32[2]{0:T(128)} %pad_add_fusion.info) | copy-start | bytes 28
  51.0 10.6 %copy-start.1 = (f32[128,768]{1,0:T(8,128)}, f32[128,768]{1,0:T(8,128)S(1)}, u32[]{:S(2)}) copy-start(f32[128,768]{1,0:T(8,128)S(1)} %get-tuple-element.45.dy_hbm.dy) | copy-start | bytes 1179652
  51.0 10.6 %all-to-all-start.2 = ((f32[8,64,128]{2,1,0:T(8,128)}), f32[8,64,128]{2,1,0:T(8,128)S(1)}, u32[]{:S(2)}, u32[]{:S(2)}) async-start(f32[8,64,128]{2,1,0:T(8,128)} %bitcast.5), calls=%async_computation.2 | async-start | bytes 524288 | tf_op jit(solution)/shard_map/all_to_all | solution.py:551
  61.6 3.8 %copy-start.6 = (f32[8,64,128]{2,1,0:T(8,128)}, f32[8,64,128]{2,1,0:T(8,128)S(1)}, u32[]{:S(2)}) copy-start(f32[8,64,128]{2,1,0:T(8,128)S(1)} %all-to-all-done.2) | copy-start | bytes 786436
  61.6 19.6 %all-to-all-start.3 = ((f32[8,240,128]{2,1,0:T(8,128)}), f32[8,240,128]{2,1,0:T(8,128)S(1)}, u32[]{:S(2)}, u32[]{:S(2)}) async-start(f32[8,240,128]{2,1,0:T(8,128)} %share.1), calls=%async_computation.3 | async-start | bytes 1966080 | tf_op jit(solution)/shard_map/all_to_all | solution.py:551
  81.2 13.2 %all-to-all-start.4 = ((f32[8,96,128]{2,1,0:T(8,128)}), f32[8,96,128]{2,1,0:T(8,128)S(1)}, u32[]{:S(2)}, u32[]{:S(2)}) async-start(f32[8,96,128]{2,1,0:T(8,128)} %attend_back.1), calls=%async_computation.4 | async-start | bytes 786432 | tf_op jit(solution)/shard_map/all_to_all | solution.py:551

commit v6 on v5

--- a/solution.py
+++ b/solution.py
@@ -96,12 +96,12 @@
 
 def key_stack(k):
     h, m, l = split3(k)
-    return jnp.concatenate([h, m, l, h, m, h], axis=1)
+    return h, jnp.concatenate([m, l, h, m, h], axis=1)
 
 
 def query_stack(q_t):
     h, m, l = split3(q_t)
-    return jnp.concatenate([h, h, h, m, m, l], axis=0)
+    return h, jnp.concatenate([h, h, m, m, l], axis=0)
 
 
 def attend_kernel(
@@ -209,11 +209,16 @@
     vh, vl = split2(jnp.transpose(qkv[:, 2 * HS:]))
     v_both = jnp.concatenate([vh, vl], axis=0)
     outs = []
-    following = dot(keys, q_t[:, :TILE])
+
+    def scores_of(c):
+        there = slice(c * TILE, (c + 1) * TILE)
+        return dot(keys[0], q_t[0][:, there]) + dot(keys[1], q_t[1][:, there])
+
+    following = scores_of(0)
     for c in range(steps):
         scores = following
         if c + 1 < steps:
-            following = dot(keys, q_t[:, (c + 1) * TILE:(c + 2) * TILE])
+            following = scores_of(c + 1)
         e = jnp.exp(scores - jnp.max(scores, axis=0, keepdims=True))
         eh, el = split2(e)
         over = 1.0 / jnp.sum(eh.astype(F32) + el.astype(F32), axis=0, keepdims=True)

time: 95.9 us -> 96.5 us (level)
  no operation moved by 1% of the time
where the time goes in v6:
time: 96.5 us; the launch traced here: 95.9 us
  Pallas kernels  40.6 us (42%)
  starting transfers between devices  23.9 us (25%)
  waiting for transfers between devices  16.6 us (17%)
  blocking collectives  10.6 us (11%)
  local copies, waits for them, and re-layouts  2.9 us (3%)
    pallas_call x1, Pallas kernels, per_device(): attend()(info, every, w_conv, w_query, w_key, w_value)  18.4 us
    pallas_call x1, Pallas kernels, per_device(): attend_back()  15.8 us
    all_to_all x3, starting transfers between devices, exchange(): lax.all_to_all(value, 'seq', 0, 0, axis_index_groups=groups, tiled=True)  12.6 us
    all_to_all x3, waiting for transfers between devices, exchange(): lax.all_to_all(value, 'seq', 0, 0, axis_index_groups=groups, tiled=True)  12 us
    all_to_all x1, blocking collectives, exchange(): lax.all_to_all(value, 'seq', 0, 0, axis_index_groups=groups, tiled=True)  10.6 us
    all_to_all x1, starting transfers between devices, per_device(): lax.all_to_all(jnp.broadcast_to(bases.reshape(1, 2, 128), (16, 2, 128)),...  8.47 us
    all_to_all x1, waiting for transfers between devices, per_device(): lax.all_to_all(jnp.broadcast_to(bases.reshape(1, 2, 128), (16, 2, 128)),...  4.58 us
    ppermute x1, starting transfers between devices, per_device(): lax.ppermute(targets, 'seq', [(i, i ^ GROUP) for i in range(2 * GROUP)])  2.83 us
  transfers between devices with their start and end apart: 5, of which 3 were waited for; matrix products, arithmetic and copies ran while one was open for 1% of the time, Pallas kernels for 20%

profile of v6, /device:TPU:16, one launch (start us, length us, event | category | flops | bytes accessed | tf_op | source)
XLA Modules:
  0.0 95.9 jit_solution(3589100312963828287)
XLA Ops:
  0.6 1.3 %broadcast_in_dim.8 = s32[16,2,128]{2,1,0:T(2,128)} broadcast(s32[2,128]{1,0:T(2,128)} %bitcast.12), dimensions={1,2} | broadcast | bytes 17408 | tf_op jit(solution)/shard_map/broadcast_in_dim | solution.py:559
  1.9 8.5 %all-to-all-start = ((s32[16,2,128]{2,1,0:T(2,128)}), s32[16,2,128]{2,1,0:T(2,128)S(1)}, u32[]{:S(2)}, u32[]{:S(2)}) async-start(s32[16,2,128]{2,1,0:T(2,128)} %broadcast_in_dim.8), calls=%async_computation | async-start | bytes 32768 | tf_op jit(solution)/shard_map/all_to_all | solution.py:559
  10.4 2.8 %collective-permute-start = (s32[64,128]{1,0:T(8,128)}, s32[64,128]{1,0:T(8,128)S(1)}, u32[]{:S(2)}, u32[]{:S(2)}) collective-permute-start(s32[64,128]{1,0:T(8,128)} %targets_here.1), channel_id=1, source_target_pairs={{0,128},{16,144},{32,160},{48,176},{64,192},{80,208},{96,224},{112... | collective-permute-start | bytes 98312 | tf_op jit(solution)/shard_map/ppermute | solution.py:558
  13.2 0.6 pad_add_fusion.info
  13.8 4.6 %all-to-all-done.bases = s32[16,2,128]{2,1,0:T(2,128)S(1)} async-done(((s32[16,2,128]{2,1,0:T(2,128)}), s32[16,2,128]{2,1,0:T(2,128)S(1)}, u32[]{:S(2)}, u32[]{:S(2)}) %all-to-all-start) | async-done | bytes 16416 | tf_op jit(solution)/shard_map/all_to_all | solution.py:559
  18.4 0.0 collective-permute-done.targets_there
  18.4 0.6 copy-done.7
  19.0 18.4 %attend.1 = (f32[128,768]{1,0:T(8,128)}, bf16[128,1024]{1,0:T(8,128)(2,1)}, f32[1,1024]{1,0:T(1,128)}, f32[512,128]{1,0:T(8,128)}, bf16[1024,768]{1,0:T(8,128)(2...) custom-call(s32[2]{0:T(128)} %pad_add_fusion.info, ...), custom_call_target="tpu_custom_call" | custom-call | tf_op jit(solution)/shard_map/attend/pallas_call | solution.py:562
  37.4 10.6 %all_to_all.37 = f32[8,64,128]{2,1,0:T(8,128)S(1)} all-to-all(f32[8,64,128]{2,1,0:T(8,128)} %bitcast.11), channel_id=1, replica_groups={{0,16,32,48,64,80,96,112},{128,144,160,176,192,208,224,240},{1,17,33,49..., dimensions={0} | all-to-all | bytes 524288 | tf_op jit(solution)/shard_map/all_to_all | solution.py:556
  48.0 0.0 copy-done.2
  48.0 1.0 %copy-done.3 = f32[128,768]{1,0:T(8,128)S(1)} copy-done((f32[128,768]{1,0:T(8,128)S(1)}, f32[128,768]{1,0:T(8,128)}, u32[]{:S(2)}) %copy-start.3) | copy-done | bytes 393240
  49.0 2.7 %decode.1 = (f32[64,128]{1,0:T(8,128)}, f32[512,128]{1,0:T(8,128)}, f32[128,768]{1,0:T(8,128)S(1)}, f32[128,768]{1,0:T(8,128)S(1)}, f32[128,128]{1,0:T(8,128)S(1)}) custom-call(f32[512,128]{1,0:T(8,128)S(1)} %bitcast.8, f32[128,768]{1,0:T(8,128)S(1)} %copy-done.3, s32[64,128]{1,0:T(8,128)S(1)} %copy-done.4, ...), custom_call_target="tpu_custom_call" | custom-call | tf_op jit(solution)/shard_map/decode/pallas_call | solution.py:564
  51.7 3.4 %all-to-all-start.2 = ((f32[8,64,128]{2,1,0:T(8,128)}), f32[8,64,128]{2,1,0:T(8,128)S(1)}, u32[]{:S(2)}, u32[]{:S(2)}) async-start(f32[8,64,128]{2,1,0:T(8,128)} %bitcast.5), calls=%async_computation.2 | async-start | bytes 524288 | tf_op jit(solution)/shard_map/all_to_all | solution.py:556
  55.1 0.0 copy-done.5
  55.1 2.2 %share.1 = f32[8,240,128]{2,1,0:T(8,128)} custom-call(s32[2]{0:T(128)S(1)} %copy-done.5, f32[512,128]{1,0:T(8,128)S(1)} %bitcast.9, f32[128,768]{1,0:T(8,128)S(1)} %get-tuple-element.45.dy_hbm.dy, f32[128,768]{1,0:T(8,128)S(1)} %get-tuple-element.51.yn_all, f32[128,128]{1,0:T(8,128)S(1)} %get-tuple-element.52.d_rate_ref), custom_call_target="tpu_custom_call" | custom-call | tf_op jit(solution)/shard_map/share/pallas_call | solution.py:566
  57.3 4.9 %all-to-all-done.2 = f32[8,64,128]{2,1,0:T(8,128)S(1)} async-done(((f32[8,64,128]{2,1,0:T(8,128)}), f32[8,64,128]{2,1,0:T(8,128)S(1)}, u32[]{:S(2)}, u32[]{:S(2)}) %all-to-all-start.2) | async-done | bytes 262176 | tf_op jit(solution)/shard_map/all_to_all | solution.py:556
  62.2 0.0 copy-done.1
  62.2 3.7 %all-to-all-start.3 = ((f32[8,240,128]{2,1,0:T(8,128)}), f32[8,240,128]{2,1,0:T(8,128)S(1)}, u32[]{:S(2)}, u32[]{:S(2)}) async-start(f32[8,240,128]{2,1,0:T(8,128)} %share.1), calls=%async_computation.3 | async-start | bytes 1966080 | tf_op jit(solution)/shard_map/all_to_all | solution.py:556
  66.0 15.8 %attend_back.1 = f32[8,96,128]{2,1,0:T(8,128)} custom-call(s32[2]{0:T(128)} %pad_add_fusion.info, f32[512,128]{1,0:T(8,128)} %bitcast.10, f32[1024,192]{1,0:T(8,128)} %get-tuple-element.40.qkv_hbm, f32[1,1024]{1,0:T(1,128)} %get-tuple-element.41.inverse, f32[192,768]{1,0:T(8,128)} %get-tuple-element.42.w_t_hbm, ...), custom_call_target="tpu_custom_call" | custom-call | tf_op jit(solution)/shard_map/attend_back/pallas_call | solution.py:567
  81.8 0.0 all-to-all-done.3.grads
  81.8 5.5 %all-to-all-start.4 = ((f32[8,96,128]{2,1,0:T(8,128)}), f32[8,96,128]{2,1,0:T(8,128)S(1)}, u32[]{:S(2)}, u32[]{:S(2)}) async-start(f32[8,96,128]{2,1,0:T(8,128)} %attend_back.1), calls=%async_computation.4 | async-start | bytes 786432 | tf_op jit(solution)/shard_map/all_to_all | solution.py:556
  87.3 0.7 add_up.1
  88.0 7.1 %all-to-all-done.4.got = f32[8,96,128]{2,1,0:T(8,128)S(1)} async-done(((f32[8,96,128]{2,1,0:T(8,128)}), f32[8,96,128]{2,1,0:T(8,128)S(1)}, u32[]{:S(2)}, u32[]{:S(2)}) %all-to-all-start.4) | async-done | bytes 393248 | tf_op jit(solution)/shard_map/all_to_all | solution.py:556
  95.0 0.8 finish.1
  (11 shorter events, 0.0 us)
Async XLA Ops:
  1.9 16.5 %all-to-all-start = ((s32[16,2,128]{2,1,0:T(2,128)}), s32[16,2,128]{2,1,0:T(2,128)S(1)}, u32[]{:S(2)}, u32[]{:S(2)}) async-start(s32[16,2,128]{2,1,0:T(2,128)} %broadcast_in_dim.8), calls=%async_computation | async-start | bytes 32768 | tf_op jit(solution)/shard_map/all_to_all | solution.py:559
  10.4 8.0 %collective-permute-start = (s32[64,128]{1,0:T(8,128)}, s32[64,128]{1,0:T(8,128)S(1)}, u32[]{:S(2)}, u32[]{:S(2)}) collective-permute-start(s32[64,128]{1,0:T(8,128)} %targets_here.1), channel_id=1, source_target_pairs={{0,128},{16,144},{32,160},{48,176},{64,192},{80,208},{96,224},{112... | collective-permute-start | bytes 98312 | tf_op jit(solution)/shard_map/ppermute | solution.py:558
  13.8 34.2 %copy-start = (f32[512,768]{1,0:T(8,128)S(1)}, f32[512,768]{1,0:T(8,128)}, u32[]{:S(2)}) copy-start(f32[512,768]{1,0:T(8,128)} %w_out.1) | copy-start | bytes 4718596
  13.8 34.2 %copy-start.2 = (f32[768,128]{1,0:T(8,128)S(1)}, f32[768,128]{1,0:T(8,128)}, u32[]{:S(2)}) copy-start(f32[768,128]{1,0:T(8,128)} %w_head.1) | copy-start | bytes 1179652
  13.8 34.2 %copy-start.4 = (s32[64,128]{1,0:T(8,128)S(1)}, s32[64,128]{1,0:T(8,128)}, u32[]{:S(2)}) copy-start(s32[64,128]{1,0:T(8,128)} %targets_here.1) | copy-start | bytes 98308
  18.4 0.6 copy-start.7
  48.0 1.0 %copy-start.3 = (f32[128,768]{1,0:T(8,128)S(1)}, f32[128,768]{1,0:T(8,128)}, u32[]{:S(2)}) copy-start(f32[128,768]{1,0:T(8,128)} %get-tuple-element.36.x_own) | copy-start | bytes 1179652
  49.0 6.1 %copy-start.5 = (s32[2]{0:T(128)S(1)}, s32[2]{0:T(128)}, u32[]{:S(2)}) copy-start(s32[2]{0:T(128)} %pad_add_fusion.info) | copy-start | bytes 28
  51.7 10.6 %copy-start.1 = (f32[128,768]{1,0:T(8,128)}, f32[128,768]{1,0:T(8,128)S(1)}, u32[]{:S(2)}) copy-start(f32[128,768]{1,0:T(8,128)S(1)} %get-tuple-element.45.dy_hbm.dy) | copy-start | bytes 1179652
  51.7 10.6 %all-to-all-start.2 = ((f32[8,64,128]{2,1,0:T(8,128)}), f32[8,64,128]{2,1,0:T(8,128)S(1)}, u32[]{:S(2)}, u32[]{:S(2)}) async-start(f32[8,64,128]{2,1,0:T(8,128)} %bitcast.5), calls=%async_computation.2 | async-start | bytes 524288 | tf_op jit(solution)/shard_map/all_to_all | solution.py:556
  62.2 3.8 %copy-start.6 = (f32[8,64,128]{2,1,0:T(8,128)}, f32[8,64,128]{2,1,0:T(8,128)S(1)}, u32[]{:S(2)}) copy-start(f32[8,64,128]{2,1,0:T(8,128)S(1)} %all-to-all-done.2) | copy-start | bytes 786436
  62.2 19.6 %all-to-all-start.3 = ((f32[8,240,128]{2,1,0:T(8,128)}), f32[8,240,128]{2,1,0:T(8,128)S(1)}, u32[]{:S(2)}, u32[]{:S(2)}) async-start(f32[8,240,128]{2,1,0:T(8,128)} %share.1), calls=%async_computation.3 | async-start | bytes 1966080 | tf_op jit(solution)/shard_map/all_to_all | solution.py:556
  81.8 13.2 %all-to-all-start.4 = ((f32[8,96,128]{2,1,0:T(8,128)}), f32[8,96,128]{2,1,0:T(8,128)S(1)}, u32[]{:S(2)}, u32[]{:S(2)}) async-start(f32[8,96,128]{2,1,0:T(8,128)} %attend_back.1), calls=%async_computation.4 | async-start | bytes 786432 | tf_op jit(solution)/shard_map/all_to_all | solution.py:556
